TPU v7x, 32 devices: a whole 2x2x4 slice. The times are simulated.
32 devices in a mesh: gx: 2 (over core), gy: 16 (over z, y, x).
Axes of the slice: x: 2, y: 2, z: 4, core: 2. Of those that a mesh axis runs over, the one named last changes fastest.
Arguments:
- velocity: float32 [2, 32, 256, 2048], P(None, None, 'gx', 'gy'), may hold values from -2.5 to 2.5
- stream_metric: float32 [256], replicated, may hold values from 0.5 to 2
- wall_metric: float32 [2048], replicated, may hold values from 0.5 to 2
Outputs:
- advection: float32 [3, 32, 256, 2048], P(None, None, 'gx', 'gy')
All inputs are finite; a program needn't handle non-finite values.
Results may differ from a plain program's by a relative error of at most 0.0003.
Values sent between devices are 32-bit elements; how exact they have to be, the bound alone decides.
No kernel may reach another device: no remote copies, remote signals or barrier semaphores. Data moves between devices by JAX's collectives and lax.ppermute only.
A program may use at most 256 MiB of HBM per device.

v0:
```python
import jax
import jax.numpy as jnp
from jax import lax
from jax.sharding import PartitionSpec as P

HIGHEST = lax.Precision.HIGHEST
CENTRAL = (0.75, -0.15, 1.0 / 60.0)
INTERIOR = (-1.0 / 60.0, 0.15, -0.75, 0.0, 0.75, -0.15, 1.0 / 60.0)
ROW_FIRST = (0.0, 0.0, 0.0, -11.0 / 6.0, 3.0, -1.5, 1.0 / 3.0)
ROW_SECOND = (0.0, 0.0, -1.0 / 3.0, -0.5, 1.0, -1.0 / 6.0, 0.0)
ROW_THIRD = (0.0, 1.0 / 12.0, -2.0 / 3.0, 0.0, 2.0 / 3.0, -1.0 / 12.0, 0.0)
ROW_SECOND_LAST = (0.0, 1.0 / 6.0, -1.0, 0.5, 1.0 / 3.0, 0.0, 0.0)
ROW_LAST = (-1.0 / 3.0, 1.5, -3.0, 11.0 / 6.0, 0.0, 0.0, 0.0)


def padded(shard, sides, width, wrap):
    for axis, dim in sides:
        devices, length = (lax.axis_size(axis), shard.shape[dim])
        up = [(i, (i + 1) % devices) for i in range(devices if wrap else devices - 1)]
        down = [(j, i) for i, j in up]
        last = lax.slice_in_dim(shard, length - width, length, axis=dim)
        first = lax.slice_in_dim(shard, 0, width, axis=dim)
        before = lax.ppermute(last, axis, up)
        after = lax.ppermute(first, axis, down)
        shard = jnp.concatenate([before, shard, after], axis=dim)
    return shard


def carried_in(part, axis, combine, identity):
    place = lax.axis_index(axis)
    gathered = lax.all_gather(part, axis)
    state = jnp.zeros_like(part) + jnp.asarray(identity, part.dtype)

    def one(lap, state):
        return combine(state, lax.dynamic_index_in_dim(gathered, lap, 0, False))

    return lax.fori_loop(0, place, one, state)


def from_root(value, axis, source):
    kept = jnp.where(lax.axis_index(axis) == source, value, 0).astype(value.dtype)
    return lax.psum(kept, axis)


def central_slope(widened, dimension, length):
    shape_out = widened.shape[:dimension] + (length,) + widened.shape[dimension + 1 :]
    result = jnp.zeros(shape_out, jnp.float32)
    for distance, weight in enumerate(CENTRAL, start=1):
        upper_part = lax.slice_in_dim(widened, 3 + distance, 3 + distance + length, axis=dimension)
        lower_part = lax.slice_in_dim(widened, 3 - distance, 3 - distance + length, axis=dimension)
        result = result + weight * (upper_part - lower_part)
    return result


def periodic_slope(values, dimension):
    result = jnp.zeros_like(values)
    for distance, weight in enumerate(CENTRAL, start=1):
        result = result + weight * (
            jnp.roll(values, -distance, axis=dimension) - jnp.roll(values, distance, axis=dimension)
        )
    return result


def row_table(global_row, rows_all):
    table = []
    for offset in range(7):
        third_rows = (global_row == 2) | (global_row == rows_all - 3)
        entry = jnp.where(
            global_row == 0,
            ROW_FIRST[offset],
            jnp.where(
                global_row == 1,
                ROW_SECOND[offset],
                jnp.where(
                    third_rows,
                    ROW_THIRD[offset],
                    jnp.where(
                        global_row == rows_all - 2,
                        ROW_SECOND_LAST[offset],
                        jnp.where(global_row == rows_all - 1, ROW_LAST[offset], INTERIOR[offset]),
                    ),
                ),
            ),
        )
        table.append(entry.astype(jnp.float32))
    return table


def wall_derivative(tall_field, table, rows_here):
    result = jnp.zeros(tall_field.shape[:-1] + (rows_here,), jnp.float32)
    for offset in range(7):
        result = result + table[offset] * tall_field[..., offset : offset + rows_here]
    return result


def add_terms(earlier, later):
    return earlier + later


def shards(velocity, stream_metric, wall_metric):
    columns = velocity.shape[2]
    rows_here = velocity.shape[3]
    columns_all = columns * lax.axis_size("gx")
    rows_all = rows_here * lax.axis_size("gy")
    column_start = lax.axis_index("gx") * columns
    row_start = lax.axis_index("gy") * rows_here
    wall_wide = padded(velocity, (("gy", 3),), 3, False)
    stream_wide = padded(velocity, (("gx", 2),), 3, True)
    margin = 0
    span_width = columns + 2 * margin
    tiled_metric = jnp.concatenate([stream_metric, stream_metric])
    metric_cols = lax.dynamic_slice_in_dim(
        tiled_metric, (column_start - margin) % columns_all, span_width
    )
    streamwise_wide = stream_wide[0]
    spanwise_wide = stream_wide[1]
    stream_grad = central_slope(streamwise_wide, 1, span_width) * metric_cols[None, :, None]
    spanwise_span = spanwise_wide[:, 3 : 3 + span_width]
    divergence = stream_grad + periodic_slope(spanwise_span, 0)
    wall_here = lax.dynamic_slice_in_dim(wall_metric, row_start, rows_here)
    slope = divergence / wall_here[None, None, :]
    row_ids = jnp.arange(rows_here, dtype=jnp.int32)
    ladder = (row_ids[:, None] <= row_ids[None, :]).astype(jnp.float32)
    climbed = jnp.einsum("zxj,jk->zxk", slope, ladder, precision=HIGHEST)
    line_sum = climbed[:, :, -1]
    below = carried_in(line_sum, "gy", add_terms, jnp.zeros_like(line_sum))
    rise_total = from_root(below + line_sum, "gy", lax.axis_size("gy") - 1)
    cell_height = 1.0 / wall_metric
    height_all = jnp.cumsum(cell_height) - 0.5 * cell_height
    fraction = lax.dynamic_slice_in_dim(height_all, row_start, rows_here) / jnp.sum(cell_height)
    rise = below[:, :, None] + climbed - 0.5 * slope
    normal = -(rise - fraction[None, None, :] * rise_total[:, :, None])
    normal_wide = padded(normal, (("gx", 1),), 3, True)
    metric_here = metric_cols[None, :, None]
    wide_fields = [streamwise_wide, normal_wide, spanwise_wide]
    stream_slopes = [stream_grad]
    for field_wide in wide_fields[1:]:
        stream_slopes.append(central_slope(field_wide, 1, columns) * metric_here)
    stream_fluxes = [
        central_slope(streamwise_wide * field_wide, 1, columns) * metric_here
        for field_wide in wide_fields
    ]
    normal_tall = padded(normal, (("gy", 2),), 3, False)
    tall_fields = [wall_wide[0], normal_tall, wall_wide[1]]
    table = row_table(row_start + row_ids, rows_all)
    normal_tall_field = tall_fields[1]
    current = [velocity[0], normal, velocity[1]]
    outputs = []
    for component in range(3):
        tall_field = tall_fields[component]
        wall_slopes = wall_derivative(tall_field, table, rows_here) * wall_here
        wall_fluxes = wall_derivative(normal_tall_field * tall_field, table, rows_here) * wall_here
        span_slopes = periodic_slope(current[component], 0)
        span_fluxes = periodic_slope(current[2] * current[component], 0)
        outputs.append(
            0.5
            * (
                current[0] * stream_slopes[component]
                + current[1] * wall_slopes
                + current[2] * span_slopes
                + stream_fluxes[component]
                + wall_fluxes
                + span_fluxes
            )
        )
    return jnp.stack(outputs)


def solution(mesh):
    in_specs = (P(None, None, "gx", "gy"), P(), P())
    out_specs = P(None, None, "gx", "gy")
    return jax.shard_map(shards, mesh=mesh, in_specs=in_specs, out_specs=out_specs, check_vma=False)
```

profile of v0, /device:TPU:8, one launch (start us, length us, event | category | flops | bytes accessed | tf_op | source)
XLA Modules:
  0.0 371.1 jit_solution(2418548078549503169)
XLA Ops:
  0.0 1.1 fusion.186
  1.2 0.5 collective-permute-start.1
  1.7 5.7 %copy.72 = f32[2,32,128,128]{2,3,1,0:T(8,128)} copy(f32[2,32,128,128]{3,2,1,0:T(8,128)} %param.5) | data formatting | bytes 8388608 | tf_op args[0]
  7.4 1.8 fusion.179
  9.2 3.4 collective-permute-start.2
  12.6 4.2 %collective-permute-start.3 = (f32[2,32,128,3]{2,3,1,0:T(4,128)}, f32[2,32,128,3]{2,3,1,0:T(4,128)}, u32[]{:S(2)}, u32[]{:S(2)}) collective-permute-start(f32[2,32,128,3]{2,3,1,0:T(4,128)} %get-tuple-element.81), channel_id=1, source_target_pairs={{1,0},{2,1},{3,2},{4,3},{5,4},{6,5},{7,6},{8,7},{9,8},{10,9},{11,1... | collective-permute-start | bytes 294920 | tf_op jit(solution)/shard_map/ppermute | solution.py:24
  16.9 7.1 %slice_bitcast_fusion.8 = (f32[31,128,128]{1,2,0:T(8,128)}, f32[31,128,128]{1,2,0:T(8,128)}, f32[31,128,128]{1,2,0:T(8,128)}, f32[31,128,128]{1,2,0:T(8,128)}) fusion(f32[2,32,128,128]{2,3,1,0:T(8,128)} %copy.72), kind=kLoop, calls=%fused_computation.267 | loop fusion | bytes 16252928 | tf_op jit(solution)/shard_map/jit(_roll_static)/slice | solution.py:59
  24.0 3.7 slice_bitcast_fusion.12
  27.7 3.7 slice_bitcast_fusion.16
  31.4 0.8 slice_bitcast_fusion.20
  32.2 0.8 slice_bitcast_fusion.24
  33.0 0.7 slice_bitcast_fusion.28
  33.7 0.6 select_select_fusion
  34.3 0.6 select_select_fusion.2
  34.9 0.6 select_select_fusion.4
  35.5 0.5 select_select_fusion.6
  36.0 0.6 fusion.177
  37.3 0.7 fusion.170
  38.1 2.7 copy.75
  40.7 2.7 copy.77
  43.4 6.8 %pad_maximum_fusion = f32[2,32,134,128]{2,3,1,0:T(8,128)S(1)} fusion(f32[2,32,3,128]{2,3,1,0:T(8,128)} %copy.77, f32[2,32,128,128]{2,3,1,0:T(8,128)} %copy.72, f32[2,32,3,128]{2,3,1,0:T(8,128)} %copy.75), kind=kLoop, calls=%fused_computation.1 | loop fusion | flops 2195456 | bytes 8781824 | tf_op jit(solution)/shard_map/concatenate | solution.py:25
  50.2 1.0 slice_bitcast_fusion.1
  51.2 2.6 copy-done.2
  53.9 1.1 fusion.185
  55.0 3.0 fusion.183
  58.0 3.0 fusion.181
  61.4 6.0 %fusion.125 = (f32[32,128,128]{1,2,0:T(8,128)S(1)}, f32[32,128,128]{1,2,0:T(8,128)}) fusion(f32[1,128,128]{1,2,0:T(8,128)S(1)} %get-tuple-element.91, f32[31,128,128]{1,2,0:T(8,128)S(1)} %get-tuple-element.93, f32[31,128,128]{1,2,0:T(8,128)S(1)} %get-tuple-element.92, f32[1,128,128]{1,2,0:T(8,128)S(1)} %get-tuple-element.90, ...), kind=kLoop, calls=%fused_computation.208 | loop fusion | flops 13107200 | bytes 29361152 | tf_op jit(solution)/shard_map/div | solution.py:121
  67.4 1.2 fusion.168
  68.8 1.3 copy-done.5
  70.1 34.8 %all-gather = f32[512,128,1]{1,2,0:T(1,128)S(1)} all-gather(f32[32,128,1]{1,2,0:T(1,128)S(1)} %slice.891), channel_id=2, replica_groups=mesh['gx'=2,'gy'=16] {'gy'}, dimensions={0}, use_global_device_ids=true | all-gather | bytes 278528 | tf_op jit(solution)/shard_map/all_gather | solution.py:31
  104.9 0.3 while.10
  105.2 71.7 %psum.7 = f32[32,128]{1,0:T(8,128)S(1)} all-reduce(f32[32,128]{1,0:T(8,128)S(1)} %add_select_fusion), channel_id=1, replica_groups=mesh['gx'=2,'gy'=16] {'gy'}, use_global_device_ids=true, to_apply=%region_5.6 | all-reduce | flops 4096 | bytes 32768 | tf_op jit(solution)/shard_map/psum | solution.py:42
  176.9 4.6 %fusion.161 = (f32[32,128,128]{1,2,0:T(8,128)S(1)}, f32[32,128,128]{1,2,0:T(8,128)S(1)}, f32[32,128,128]{1,2,0:T(8,128)S(1)}, f32[32,128,128]{1,2,0:T(8,128)S(1)}) fusion(f32[2,32,128,128]{2,3,1,0:T(8,128)} %copy.72, f32[32,128]{1,0:T(8,128)S(1)} %psum.7, f32[128]{0:T(128)S(1)} %fusion.170, f32[32,128,128]{1,2,0:T(8,128)} %copy-done.4, ...), kind=kLoop, calls=%fused_computation.277 | loop fusion | flops 4718592 | bytes 16810496 | tf_op jit(solution)/shard_map/mul | solution.py:154
  181.5 3.5 fusion.192
  185.0 3.4 fusion.190
  188.5 3.4 fusion.188
  191.8 0.8 fusion.187
  192.6 0.8 fusion.189
  193.5 0.7 fusion.191
  194.2 2.7 fusion.205
  196.9 3.5 fusion.204
  200.4 3.4 fusion.202
  203.7 3.3 fusion.200
  207.0 0.8 fusion.199
  207.8 0.8 fusion.201
  208.6 0.7 fusion.203
  209.3 2.8 copy.95
  212.1 2.8 copy.97
  215.0 0.5 collective-permute-start.7
  215.5 2.7 pad_maximum_fusion.2
  218.2 2.5 slice_bitcast_fusion.3
  220.7 0.9 copy-done.3
  221.6 0.7 fusion.212
  222.3 1.9 collective-permute-start.4
  224.2 5.9 %collective-permute-start.5 = (f32[32,128,3]{1,2,0:T(4,128)}, f32[32,128,3]{1,2,0:T(4,128)}, u32[]{:S(2)}, u32[]{:S(2)}) collective-permute-start(f32[32,128,3]{1,2,0:T(4,128)} %get-tuple-element.148), channel_id=1, source_target_pairs={{1,0},{2,1},{3,2},{4,3},{5,4},{6,5},{7,6},{8,7},{9,8},{10,9},{11,1... | collective-permute-start | bytes 147464 | tf_op jit(solution)/shard_map/ppermute | solution.py:24
  230.2 2.8 copy.96
  232.9 2.7 copy.98
  235.7 8.4 %fusion.176 = (f32[32,134,128]{1,2,0:T(8,128)}, f32[32,134,128]{1,2,0:T(8,128)}, f32[32,134,128]{1,2,0:T(8,128)}) fusion(f32[2,32,134,128]{2,3,1,0:T(8,128)} %copy-done.2, f32[32,3,128]{1,2,0:T(8,128)} %copy.96, f32[32,128,128]{1,2,0:T(8,128)S(1)} %get-tuple-element.55, f32[32,3,128]{1,2,0:T(8,128)} %copy.98), kind=kLoop, calls=%fused_computation.320 | loop fusion | flops 2744320 | bytes 13172736 | tf_op jit(solution)/shard_map/mul | solution.py:140
  244.2 5.5 %fusion.166 = (f32[32,128,134]{1,2,0:T(8,128)}, f32[32,128,134]{1,2,0:T(8,128)}, f32[32,128,134]{1,2,0:T(8,128)}) fusion(f32[32,128,3]{1,2,0:T(4,128)} %collective-permute-done.5, f32[32,128,128]{1,2,0:T(8,128)S(1)} %get-tuple-element.55, f32[32,128,3]{1,2,0:T(4,128)S(1)} %collective-permute-done.4, f32[2,32,128,134]{2,3,1,0:T(8,128)} %copy-done.3), kind=kLoop, calls=%fused_computation.282 | loop fusion | flops 2744320 | bytes 13172736 | tf_op jit(solution)/shard_map/mul | solution.py:152
  249.6 40.5 %fusion.40 = f32[1,32,128,128]{2,3,1,0:T(8,128)} fusion(f32[32,128,134]{1,2,0:T(8,128)} %get-tuple-element.49, f32[32,134,128]{1,2,0:T(8,128)} %get-tuple-element.45, f32[32,128,128]{1,2,0:T(8,128)S(1)} %get-tuple-element.55, f32[32,128,134]{1,2,0:T(8,128)} %get-tuple-element.51, f32[32,134,128]{1,2,0:T(8,128)} %copy-done.1, ...), kind=kLoop, calls=%fused_computation.67 | loop fusion | flops 43515904 | bytes 88084992 | tf_op jit(solution)/shard_map/stack | solution.py:166
  290.2 34.6 %fusion.92 = f32[1,32,128,128]{2,3,1,0:T(8,128)} fusion(f32[32,128,134]{1,2,0:T(8,128)} %get-tuple-element.48, f32[32,134,128]{1,2,0:T(8,128)} %get-tuple-element.43, f32[32,128,128]{1,2,0:T(8,128)S(1)} %get-tuple-element.55, f32[32,128,134]{1,2,0:T(8,128)} %get-tuple-element.50, f32[1,128,128]{1,2,0:T(8,128)} %get-tuple-element.75, ...), kind=kLoop, calls=%fused_computation.153 | loop fusion | flops 38797312 | bytes 77599232 | tf_op jit(solution)/shard_map/stack | solution.py:166
  324.9 33.3 %fusion.12 = f32[1,32,128,128]{2,3,1,0:T(8,128)} fusion(f32[32,128,128]{1,2,0:T(8,128)S(1)} %get-tuple-element.55, f32[32,128,3]{1,2,0:T(4,128)} %collective-permute-done.5, f32[32,128,3]{1,2,0:T(4,128)S(1)} %collective-permute-done.4, f32[32,3,128]{1,2,0:T(8,128)} %copy.98, f32[32,3,128]{1,2,0:T(8,128)} %copy.96, f32[32,128,134]{1,2,0:T(8,128)} %get-tuple-element.96, ...), kind=kLoop, calls=%fused_computation.38 | loop fusion | flops 49807360 | bytes 61018624 | tf_op jit(solution)/shard_map/stack | solution.py:166
  358.2 6.3 %pad_maximum_fusion.1 = f32[3,32,128,128]{2,3,1,0:T(8,128)} fusion(f32[1,32,128,128]{2,3,1,0:T(8,128)} %fusion.40, f32[1,32,128,128]{2,3,1,0:T(8,128)} %fusion.12, f32[1,32,128,128]{2,3,1,0:T(8,128)} %fusion.92), kind=kLoop, calls=%fused_computation.2 | loop fusion | flops 3145728 | bytes 12582912 | tf_op jit(solution)/shard_map/stack | solution.py:166
  364.6 6.6 %copy.113 = f32[3,32,128,128]{3,2,1,0:T(8,128)} copy(f32[3,32,128,128]{2,3,1,0:T(8,128)} %pad_maximum_fusion.1) | data formatting | bytes 12582912 | tf_op jit(solution)/shard_map/stack | solution.py:166
  (73 shorter events, 1.5 us)
Async XLA Ops:
  1.1 37.0 %collective-permute-start = (f32[2,32,3,128]{3,1,2,0:T(8,128)S(1)}, f32[2,32,3,128]{3,1,2,0:T(8,128)S(1)}, u32[]{:S(2)}, u32[]{:S(2)}) collective-permute-start(f32[2,32,3,128]{3,1,2,0:T(8,128)S(1)} %copy.115), channel_id=1, source_target_pairs={{0,16},{16,0},{1,17},{17,1},{2,18},{18,2},{3,19},{19,3},{4,20},{20... | collective-permute-start | bytes 294920 | tf_op jit(solution)/shard_map/ppermute | solution.py:23
  1.2 39.5 %collective-permute-start.1 = (f32[2,32,3,128]{3,1,2,0:T(8,128)S(1)}, f32[2,32,3,128]{3,1,2,0:T(8,128)S(1)}, u32[]{:S(2)}, u32[]{:S(2)}) collective-permute-start(f32[2,32,3,128]{3,1,2,0:T(8,128)S(1)} %copy.116), channel_id=1, source_target_pairs={{16,0},{0,16},{17,1},{1,17},{18,2},{2,18},{19,3},{3,19},{20,4},{4,... | collective-permute-start | bytes 294920 | tf_op jit(solution)/shard_map/ppermute | solution.py:24
  9.2 206.2 %collective-permute-start.2 = (f32[2,32,128,3]{2,3,1,0:T(4,128)}, f32[2,32,128,3]{2,3,1,0:T(4,128)}, u32[]{:S(2)}, u32[]{:S(2)}) collective-permute-start(f32[2,32,128,3]{2,3,1,0:T(4,128)} %get-tuple-element.80), channel_id=1, source_target_pairs={{0,1},{1,2},{2,3},{3,4},{4,5},{5,6},{6,7},{7,8},{8,9},{9,10},{10,1... | collective-permute-start | bytes 294920 | tf_op jit(solution)/shard_map/ppermute | solution.py:23
  12.6 202.8 %collective-permute-start.3 = (f32[2,32,128,3]{2,3,1,0:T(4,128)}, f32[2,32,128,3]{2,3,1,0:T(4,128)}, u32[]{:S(2)}, u32[]{:S(2)}) collective-permute-start(f32[2,32,128,3]{2,3,1,0:T(4,128)} %get-tuple-element.81), channel_id=1, source_target_pairs={{1,0},{2,1},{3,2},{4,3},{5,4},{6,5},{7,6},{8,7},{9,8},{10,9},{11,1... | collective-permute-start | bytes 294920 | tf_op jit(solution)/shard_map/ppermute | solution.py:24
  16.9 7.1 %copy-start = (f32[2,32,128,128]{2,3,1,0:T(8,128)S(1)}, f32[2,32,128,128]{2,3,1,0:T(8,128)}, u32[]{:S(2)}) copy-start(f32[2,32,128,128]{2,3,1,0:T(8,128)} %copy.72) | copy-start | bytes 12582916
  31.4 4.6 %copy-start.22 = (f32[256]{0:T(256)S(1)}, f32[256]{0:T(256)}, u32[]{:S(2)}) copy-start(f32[256]{0:T(256)} %param.6) | copy-start | bytes 3076
  31.4 4.6 %copy-start.17 = (f32[2048]{0:T(1024)S(1)}, f32[2048]{0:T(1024)}, u32[]{:S(2)}) copy-start(f32[2048]{0:T(1024)} %param.7) | copy-start | bytes 24580
  36.7 24.7 %copy-start.11 = (f32[128]{0:T(128)}, f32[128]{0:T(128)S(1)}, u32[]{:S(2)}) copy-start(f32[128]{0:T(128)S(1)} %dynamic_slice.14) | copy-start | bytes 1540
  37.3 24.1 %copy-start.14 = (f32[128]{0:T(128)}, f32[128]{0:T(128)S(1)}, u32[]{:S(2)}) copy-start(f32[128]{0:T(128)S(1)} %dynamic_slice.13) | copy-start | bytes 1540
  50.2 3.7 copy-start.2
  53.9 7.4 %copy-start.1 = (f32[32,134,128]{1,2,0:T(8,128)}, f32[32,134,128]{1,2,0:T(8,128)S(1)}, u32[]{:S(2)}) copy-start(f32[32,134,128]{1,2,0:T(8,128)S(1)} %get-tuple-element.47) | copy-start | bytes 6586372
  67.4 1.3 copy-start.4
  68.8 1.3 copy-start.5
  212.1 18.0 %collective-permute-start.6 = (f32[32,3,128]{2,0,1:T(8,128)}, f32[32,3,128]{2,0,1:T(8,128)}, u32[]{:S(2)}, u32[]{:S(2)}) collective-permute-start(f32[32,3,128]{2,0,1:T(8,128)} %copy.95), channel_id=1, source_target_pairs={{16,0},{0,16},{17,1},{1,17},{18,2},{2,18},{19,3},{3,19},{20,4},{4,... | collective-permute-start | bytes 147464 | tf_op jit(solution)/shard_map/ppermute | solution.py:24
  215.0 18.0 %collective-permute-start.7 = (f32[32,3,128]{2,0,1:T(8,128)}, f32[32,3,128]{2,0,1:T(8,128)}, u32[]{:S(2)}, u32[]{:S(2)}) collective-permute-start(f32[32,3,128]{2,0,1:T(8,128)} %copy.97), channel_id=1, source_target_pairs={{0,16},{16,0},{1,17},{17,1},{2,18},{18,2},{3,19},{19,3},{4,20},{20... | collective-permute-start | bytes 147464 | tf_op jit(solution)/shard_map/ppermute | solution.py:23
  218.2 3.4 copy-start.3
  222.3 21.9 %collective-permute-start.4 = (f32[32,128,3]{1,2,0:T(4,128)}, f32[32,128,3]{1,2,0:T(4,128)S(1)}, u32[]{:S(2)}, u32[]{:S(2)}) collective-permute-start(f32[32,128,3]{1,2,0:T(4,128)} %get-tuple-element.147), channel_id=1, source_target_pairs={{0,1},{1,2},{2,3},{3,4},{4,5},{5,6},{6,7},{7,8},{8,9},{9,10},{10,1... | collective-permute-start | bytes 147464 | tf_op jit(solution)/shard_map/ppermute | solution.py:23
  224.2 19.9 %collective-permute-start.5 = (f32[32,128,3]{1,2,0:T(4,128)}, f32[32,128,3]{1,2,0:T(4,128)}, u32[]{:S(2)}, u32[]{:S(2)}) collective-permute-start(f32[32,128,3]{1,2,0:T(4,128)} %get-tuple-element.148), channel_id=1, source_target_pairs={{1,0},{2,1},{3,2},{4,3},{5,4},{6,5},{7,6},{8,7},{9,8},{10,9},{11,1... | collective-permute-start | bytes 147464 | tf_op jit(solution)/shard_map/ppermute | solution.py:24
  244.1 5.5 %copy-start.12 = (f32[128]{0:T(128)S(1)}, f32[128]{0:T(128)}, u32[]{:S(2)}) copy-start(f32[128]{0:T(128)} %copy-done.11) | copy-start | bytes 1540
  244.1 5.5 %copy-start.15 = (f32[128]{0:T(128)S(1)}, f32[128]{0:T(128)}, u32[]{:S(2)}) copy-start(f32[128]{0:T(128)} %copy-done.14) | copy-start | bytes 1540
  244.1 5.5 %copy-start.18 = (f32[128]{0:T(128)S(1)}, f32[128]{0:T(128)}, u32[]{:S(2)}) copy-start(f32[128]{0:T(128)} %get-tuple-element.149) | copy-start | bytes 1540
  244.1 5.5 %copy-start.20 = (f32[128]{0:T(128)S(1)}, f32[128]{0:T(128)}, u32[]{:S(2)}) copy-start(f32[128]{0:T(128)} %get-tuple-element.150) | copy-start | bytes 1540
  290.1 34.6 %copy-start.6 = (f32[2,128,128]{1,2,0:T(8,128)S(1)}, f32[2,128,128]{1,2,0:T(8,128)}, u32[]{:S(2)}) copy-start(f32[2,128,128]{1,2,0:T(8,128)} %get-tuple-element.159) | copy-start | bytes 393220
  290.2 34.6 %copy-start.7 = (f32[2,128,128]{1,2,0:T(8,128)S(1)}, f32[2,128,128]{1,2,0:T(8,128)}, u32[]{:S(2)}) copy-start(f32[2,128,128]{1,2,0:T(8,128)} %get-tuple-element.160) | copy-start | bytes 393220
  290.2 34.6 %copy-start.8 = (f32[2,128,128]{1,2,0:T(8,128)S(1)}, f32[2,128,128]{1,2,0:T(8,128)}, u32[]{:S(2)}) copy-start(f32[2,128,128]{1,2,0:T(8,128)} %get-tuple-element.125) | copy-start | bytes 393220
  290.2 34.6 %copy-start.9 = (f32[2,128,128]{1,2,0:T(8,128)S(1)}, f32[2,128,128]{1,2,0:T(8,128)}, u32[]{:S(2)}) copy-start(f32[2,128,128]{1,2,0:T(8,128)} %get-tuple-element.126) | copy-start | bytes 393220
  290.2 34.6 %copy-start.10 = (f32[1,128,128]{1,2,0:T(8,128)S(1)}, f32[1,128,128]{1,2,0:T(8,128)}, u32[]{:S(2)}) copy-start(f32[1,128,128]{1,2,0:T(8,128)} %get-tuple-element.163) | copy-start | bytes 196612
  290.2 34.6 %copy-start.13 = (f32[128]{0:T(128)S(1)}, f32[128]{0:T(128)}, u32[]{:S(2)}) copy-start(f32[128]{0:T(128)} %copy-done.11) | copy-start | bytes 1540
  290.2 34.6 %copy-start.16 = (f32[128]{0:T(128)S(1)}, f32[128]{0:T(128)}, u32[]{:S(2)}) copy-start(f32[128]{0:T(128)} %copy-done.14) | copy-start | bytes 1540
  290.2 34.6 %copy-start.19 = (f32[128]{0:T(128)S(1)}, f32[128]{0:T(128)}, u32[]{:S(2)}) copy-start(f32[128]{0:T(128)} %get-tuple-element.149) | copy-start | bytes 1540
  290.2 34.6 %copy-start.21 = (f32[128]{0:T(128)S(1)}, f32[128]{0:T(128)}, u32[]{:S(2)}) copy-start(f32[128]{0:T(128)} %get-tuple-element.150) | copy-start | bytes 1540
where the time goes:
time: 374 us; the launch traced here: 371 us
  other arithmetic  153 us (41%)
  blocking collectives  106 us (28%)
  local copies, waits for them, and re-layouts  93.3 us (25%)
  starting transfers between devices  16.6 us (4%)
    another operation x4, other arithmetic, shards(): return jnp.stack(outputs)  115 us
    psum x1, blocking collectives, from_root(): return lax.psum(kept, axis)  71.7 us
    slice x24, local copies, waits for them, and re-layouts, periodic_slope(): jnp.roll(values, distance, axis=dimension)  49.3 us
    all_gather x1, blocking collectives, carried_in(): gathered = lax.all_gather(part, axis)  34.8 us
    unnamed x49, local copies, waits for them, and re-layouts  10.8 us
    ppermute x4, starting transfers between devices, padded(): after = lax.ppermute(first, axis, down)  10.7 us
    concatenate x2, other arithmetic, padded(): shard = jnp.concatenate([before, shard, after], axis=dim)  9.48 us
    mul x1, other arithmetic, shards(): streamwise_wide * field_wide  8.43 us
  transfers between devices with their start and end apart: 8, of which 0 were waited for; matrix products, arithmetic and copies ran while one was open for 31% of the time, Pallas kernels for 0%

commit v1 on v0

v1 whole, which is shorter than its diff:
```python
import jax
import jax.numpy as jnp
from jax import lax
from jax.experimental import pallas as pl
from jax.experimental.pallas import tpu as pltpu
from jax.sharding import PartitionSpec as P

F32 = jnp.float32
BF16 = jnp.bfloat16
HALF60 = 0.5 / 60.0
CENTRAL = ((1, 45.0), (2, -9.0), (3, 1.0))
WALL_ROWS = (
    {0: -110.0, 1: 180.0, 2: -90.0, 3: 20.0},
    {-1: -20.0, 0: -30.0, 1: 60.0, 2: -10.0},
    {-2: 5.0, -1: -40.0, 1: 40.0, 2: -5.0},
)
LANES = 128
EDGE = 8
LOW = EDGE - 3

WHOLE = pl.BlockSpec(memory_space=pltpu.VMEM)
ANY = pl.BlockSpec(memory_space=pl.ANY)


def iota(shape, dim):
    return lax.broadcasted_iota(jnp.int32, shape, dim)


def split(value):
    high = value.astype(BF16)
    low = (value - high.astype(F32)).astype(BF16)
    return jnp.concatenate([high, low], axis=1)


def wrapped(plane, nz):
    return lax.rem(plane + nz, nz)


def wall_matrix(place, last):
    h = iota((LANES, LANES), 0)
    j = iota((LANES, LANES), 1)
    away = h - j
    inner = jnp.zeros((LANES, LANES), F32)
    for distance, weight in CENTRAL:
        inner = jnp.where(away == distance, weight, inner)
        inner = jnp.where(away == -distance, -weight, inner)
    for row, entries in enumerate(WALL_ROWS):
        for side in (0, 1):
            at = row if side == 0 else LANES - 1 - row
            sign = 1 if side == 0 else -1
            closed = jnp.zeros((LANES, LANES), F32)
            for offset, weight in entries.items():
                closed = jnp.where(away == sign * offset, sign * weight, closed)
            here = jnp.where(place == (0 if side == 0 else last), 1, 0)
            inner = jnp.where((j == at) & (here == 1), closed, inner)
    inner = inner.astype(BF16)
    return jnp.concatenate([inner, inner], axis=0)


def prepare(nz, vel, xr, metric, wall, pad, v0, strip_a, strip_b, sums, mh, ms, slope_s, turned, sems):
    gx = lax.axis_index("gx")
    gy = lax.axis_index("gy")
    columns = metric.shape[1]
    chunks = 8
    per = nz // chunks

    def chunk(c):
        planes = pl.ds(c * per, per)
        return pltpu.make_async_copy(vel.at[:, planes], pad.at[:, planes, pl.ds(EDGE, columns)], sems.at[c])

    for c in range(chunks):
        chunk(c).start()
    right = pltpu.make_async_copy(xr.at[:, :, pl.ds(0, EDGE)], pad.at[:, :, pl.ds(EDGE + columns, EDGE)], sems.at[chunks])
    left = pltpu.make_async_copy(xr.at[:, :, pl.ds(EDGE, EDGE)], pad.at[:, :, pl.ds(0, EDGE)], sems.at[chunks + 1])
    right.start()
    left.start()

    own = jnp.broadcast_to(metric[pl.ds(gx, 1), :], (LANES, columns)).T
    peer = jnp.broadcast_to(metric[pl.ds(1 - gx, 1), :], (LANES, columns)).T
    ms[0:EDGE, :] = peer[columns - EDGE :]
    ms[EDGE : EDGE + columns, :] = own
    ms[EDGE + columns :, :] = peer[:EDGE]
    mh[...] = ms[...] * HALF60
    rw60 = 1.0 / (60.0 * wall[pl.ds(gy, 1), :])
    h = iota((LANES, LANES), 0)
    j = iota((LANES, LANES), 1)
    climb = jnp.where(h < j, -1.0, jnp.where(h == j, -0.5, 0.0)).astype(BF16)
    climb = jnp.concatenate([climb, jnp.ones((LANES, LANES), BF16)], axis=1)
    climb = jnp.concatenate([climb, climb], axis=0)
    rows = columns + EDGE
    lane = iota((rows, LANES), 1)
    lane_c = iota((columns, LANES), 1)
    odd = lax.rem(gy, 2) == 1
    sums[...] = jnp.zeros((rows, LANES), F32)
    right.wait()
    left.wait()
    chunk(0).wait()
    chunk(1).wait()

    def plane(step, _):
        z = lax.rem(step, nz)
        ups = [wrapped(z + d, nz) for d in (1, 2, 3)]
        downs = [wrapped(z - d, nz) for d in (1, 2, 3)]
        blocks = []
        for k in range(rows // 8):
            r = LOW + 8 * k
            du = dw = None
            for distance, weight in CENTRAL:
                a = pad[0, z, pl.ds(r + distance, 8), :] - pad[0, z, pl.ds(r - distance, 8), :]
                b = pad[1, ups[distance - 1], pl.ds(r, 8), :] - pad[1, downs[distance - 1], pl.ds(r, 8), :]
                if weight != 1.0:
                    a, b = weight * a, weight * b
                du = a if du is None else du + a
                dw = b if dw is None else dw + b
            slope = (ms[pl.ds(r, 8), :] * du + dw) * rw60
            slope_s[pl.ds(8 * k, 8), :] = slope
            blocks.append(slope)
        result = jnp.dot(split(jnp.concatenate(blocks, axis=0)), climb, preferred_element_type=F32)
        v0[z, pl.ds(LOW, rows), :] = result[:, :LANES]
        sums[...] = jnp.where(lane == z, result[:, LANES:], sums[...])
        packed = jnp.where(
            lane_c < 6,
            pltpu.roll(pad[0, z, pl.ds(EDGE, columns), :], 3, 1),
            jnp.where(
                lane_c < 12,
                pltpu.roll(pad[1, z, pl.ds(EDGE, columns), :], 9, 1),
                pltpu.roll(slope_s[pl.ds(3, columns), :], 15, 1),
            ),
        )
        turned[...] = packed.T[:24]
        for f in range(3):
            last = turned[6 * f : 6 * f + 3, :]
            first = turned[6 * f + 3 : 6 * f + 6, :]
            strip_a[pl.ds(3 * f * nz + z, 3, stride=nz), :] = jnp.where(odd, first, last)
            strip_b[pl.ds(3 * f * nz + z, 3, stride=nz), :] = jnp.where(odd, last, first)
        return 0

    def group(g, _):
        @pl.when(g < chunks - 2)
        def _():
            chunk(g + 2).wait()

        return lax.fori_loop(per * g + 3, per * g + 3 + per, plane, 0)

    lax.fori_loop(0, chunks, group, 0)


def stream_terms(nz, pad, mh, part, gx_out):
    columns = part.shape[2]

    def plane(z, _):
        for k in range(-1, columns // 8):
            r = EDGE + 8 * k
            u = pad[0, z, pl.ds(r, 8), :]
            total = [None, None]
            for distance, weight in CENTRAL:
                g = u + pad[0, z, pl.ds(r + distance, 8), :]
                if weight != 1.0:
                    g = weight * g
                gx_out[distance - 1, z, pl.ds(r, 8), :] = g
                if k < 0:
                    continue
                g_low = gx_out[distance - 1, z, pl.ds(r - distance, 8), :]
                for c in range(2):
                    term = g * pad[c, z, pl.ds(r + distance, 8), :] - g_low * pad[c, z, pl.ds(r - distance, 8), :]
                    total[c] = term if total[c] is None else total[c] + term
            if k >= 0:
                for c in range(2):
                    part[c, z, pl.ds(8 * k, 8), :] = total[c] * mh[pl.ds(r, 8), :]
        return 0

    lax.fori_loop(0, nz, plane, 0)


def span_terms(nz, pad, part, out, gz_out):
    columns = part.shape[2]

    def factors(z, k):
        r = EDGE + 8 * k
        w = pad[1, z, pl.ds(r, 8), :]
        made = []
        for distance, weight in CENTRAL:
            g = (w + pad[1, wrapped(z + distance, nz), pl.ds(r, 8), :]) * (weight * HALF60)
            gz_out[distance - 1, z, pl.ds(8 * k, 8), :] = g
            made.append(g)
        return made

    def first(z, _):
        for k in range(columns // 8):
            factors(z, k)
        return 0

    def plane(z, _):
        for k in range(columns // 8):
            r = EDGE + 8 * k
            made = factors(z, k)
            total = [part[c, z, pl.ds(8 * k, 8), :] for c in range(2)]
            for distance, _w in CENTRAL:
                up, down = wrapped(z + distance, nz), wrapped(z - distance, nz)
                g_low = gz_out[distance - 1, down, pl.ds(8 * k, 8), :]
                for c in range(2):
                    total[c] = total[c] + (made[distance - 1] * pad[c, up, pl.ds(r, 8), :] - g_low * pad[c, down, pl.ds(r, 8), :])
            for c in range(2):
                out[c, z, pl.ds(8 * k, 8), :] = total[c]
        return 0

    lax.fori_loop(nz - 3, nz, first, 0)
    lax.fori_loop(0, nz, plane, 0)


def wall_terms(nz, last, pad, wall, out):
    gy = lax.axis_index("gy")
    columns = out.shape[2]
    matrix = wall_matrix(gy, last)
    scale = wall[pl.ds(gy, 1), :] * HALF60

    def plane(z, _):
        for c in range(2):
            value = pad[c, z, pl.ds(EDGE, columns), :]
            out[c, z] = jnp.dot(split(value), matrix, preferred_element_type=F32) * scale
        return 0

    lax.fori_loop(0, nz, plane, 0)


def heights(wall, block, blocks):
    cell = 1.0 / wall[...]
    row = iota(cell.shape, 0)
    total = jnp.sum(cell)
    before = jnp.sum(jnp.where(row < block, cell, 0.0))
    mine = 1.0 / wall[pl.ds(block, 1), :]
    prefix = mine
    lane = iota((1, LANES), 1)
    for shift in (1, 2, 4, 8, 16, 32, 64):
        prefix = prefix + jnp.where(lane >= shift, pltpu.roll(prefix, shift, 1), 0.0)
    return (before + prefix - 0.5 * mine) / total


def finish(nz, last, pad, v0, part, dwall, gxs, gzs, mh, wall, own_a, own_b, got_a, got_b, below, total, sums, out, v, buf, fixes, lhs, sems):
    gy = lax.axis_index("gy")
    columns = buf.shape[2]
    rows = columns + EDGE
    odd = lax.rem(gy, 2) == 1
    matrix = wall_matrix(gy, last)
    scale = wall[pl.ds(gy, 1), :] * HALF60
    frac = heights(wall, gy, last + 1)
    frac_low = heights(wall, jnp.maximum(gy - 1, 0), last + 1)
    frac_high = heights(wall, jnp.minimum(gy + 1, last), last + 1)

    def strip(pick, f, r):
        at = pl.ds((3 * f + r) * nz, nz)
        return pick[0][at, :], pick[1][at, :]

    def own_first(f, r):
        a, b = strip((own_a, own_b), f, r)
        return jnp.where(odd, a, b)

    def own_last(f, r):
        a, b = strip((own_a, own_b), f, r)
        return jnp.where(odd, b, a)

    def from_low(f, r):
        a, b = strip((got_a, got_b), f, r)
        return jnp.where(odd, a, b)

    def from_high(f, r):
        a, b = strip((got_a, got_b), f, r)
        return jnp.where(odd, b, a)

    def compact(ref):
        return ref[pl.ds(3, columns), :].T[:nz]

    below_c = compact(below)
    total_c = compact(total)
    incl_c = below_c + compact(sums)
    lane_one = lambda vector, at: vector[:, at : at + 1]

    def climb(start, slopes, sign, fractions):
        level, made = start, []
        for slope, fraction in zip(slopes, fractions):
            made.append(fraction * total_c - (level + (0.5 * sign) * slope))
            level = level + sign * slope
        return made

    v_first = climb(below_c, [own_first(2, r) for r in range(3)], 1.0, [lane_one(frac, r) for r in range(3)])
    v_last = climb(incl_c, [own_last(2, 2 - q) for q in range(3)], -1.0, [lane_one(frac, LANES - 1 - q) for q in range(3)])
    v_low = climb(below_c, [from_low(2, 2 - q) for q in range(3)], -1.0, [lane_one(frac_low, LANES - 1 - q) for q in range(3)])
    v_high = climb(incl_c, [from_high(2, r) for r in range(3)], 1.0, [lane_one(frac_high, r) for r in range(3)])
    v_low = [jnp.where(gy > 0, x, 0.0) for x in v_low]
    v_high = [jnp.where(gy < last, x, 0.0) for x in v_high]
    weight_of = dict(CENTRAL)
    for i in range(24):
        if i % 8 >= 6:
            fixes[pl.ds(i * nz, nz), :] = jnp.zeros((nz, LANES), F32)
    for c in range(3):
        for side in range(2):
            v_own, v_out = (v_first, v_low) if side == 0 else (v_last, v_high)
            for q in range(3):
                value = None
                for m in range(3 - q):
                    if c == 1:
                        field = v_out[m]
                    elif side == 0:
                        field = from_low(c // 2, 2 - m)
                    else:
                        field = from_high(c // 2, m)
                    weight = weight_of[q + m + 1] * (-1.0 if side == 0 else 1.0)
                    term = weight * ((v_own[q] + v_out[m]) * field)
                    value = term if value is None else value + term
                slot = 3 + q if side == 0 else 2 - q
                at = q if side == 0 else LANES - 1 - q
                fixes[pl.ds((8 * c + slot) * nz, nz), :] = value * lane_one(scale, at)

    below_v = below[...]
    total_v = total[...]
    below_h = below_v.astype(BF16).astype(F32)
    below_l = below_v - below_h
    total_h = total_v.astype(BF16).astype(F32)
    total_l = total_v - total_h
    quarter = iota((rows, LANES), 1) // nz
    first_half = jnp.where(
        quarter == 0,
        below_h,
        jnp.where(
            quarter == 1,
            pltpu.roll(below_l, nz, 1),
            jnp.where(quarter == 2, pltpu.roll(total_h, 2 * nz, 1), pltpu.roll(total_l, 3 * nz, 1)),
        ),
    )
    second_half = jnp.where(quarter == 0, total_h, jnp.where(quarter == 1, pltpu.roll(total_l, nz, 1), 0.0))
    lhs[:, :LANES] = first_half.astype(BF16)
    lhs[:, LANES:] = second_half.astype(BF16)
    frac_h = frac.astype(BF16).astype(F32)
    frac_l = frac - frac_h
    k_index = iota((2 * LANES, LANES), 0)
    base = jnp.where(
        k_index < 2 * nz,
        -1.0,
        jnp.where(k_index < LANES, jnp.broadcast_to(frac_h, (2 * LANES, LANES)), jnp.broadcast_to(frac_l, (2 * LANES, LANES))),
    )
    k_plane = lax.rem(k_index, nz)

    def make_v(step):
        z = wrapped(step, nz)
        chosen = jnp.where(k_plane == z, base, 0.0).astype(BF16)
        v[z, pl.ds(LOW, rows), :] = v0[z, pl.ds(LOW, rows), :] + jnp.dot(lhs[...], chosen, preferred_element_type=F32)

    def make_first(step, _):
        make_v(step)
        return 0

    lax.fori_loop(nz - 3, nz + 4, make_first, 0)
    lane = iota((columns, LANES), 1)
    at_edge = (lane < 3) | (lane >= LANES - 3)
    zeros = jnp.zeros((LANES - 24, LANES), F32)
    chunks = 8
    per = nz // chunks

    def plane(z, _):
        @pl.when(z < nz - 7)
        def _():
            make_v(z + 4)

        turned = jnp.concatenate([fixes[pl.ds(z, 24, stride=nz), :], zeros], axis=0).T
        fix = [jnp.where(at_edge, pltpu.roll(turned, LANES - 3 - 8 * c, 1), 0.0) for c in range(3)]
        here = v[z, pl.ds(EDGE, columns), :]
        d_v = jnp.dot(split(here), matrix, preferred_element_type=F32)
        d_vv = jnp.dot(split(here * here), matrix, preferred_element_type=F32)
        d_vu = jnp.dot(split(here * pad[0, z, pl.ds(EDGE, columns), :]), matrix, preferred_element_type=F32)
        d_vw = jnp.dot(split(here * pad[1, z, pl.ds(EDGE, columns), :]), matrix, preferred_element_type=F32)
        buf[0, z] = part[0, z] + here * dwall[0, z] + (scale * d_vu + fix[0])
        buf[2, z] = part[1, z] + here * dwall[1, z] + (scale * d_vw + fix[2])
        for k in range(columns // 8):
            r = EDGE + 8 * k
            at = pl.ds(8 * k, 8)
            across = along = None
            for distance, _w in CENTRAL:
                up, down = wrapped(z + distance, nz), wrapped(z - distance, nz)
                a = gxs[distance - 1, z, pl.ds(r, 8), :] * v[z, pl.ds(r + distance, 8), :]
                a = a - gxs[distance - 1, z, pl.ds(r - distance, 8), :] * v[z, pl.ds(r - distance, 8), :]
                b = gzs[distance - 1, z, at, :] * v[up, pl.ds(r, 8), :]
                b = b - gzs[distance - 1, down, at, :] * v[down, pl.ds(r, 8), :]
                across = a if across is None else across + a
                along = b if along is None else along + b
            rows_k = slice(8 * k, 8 * k + 8)
            wallward = scale * (here[rows_k] * d_v[rows_k] + d_vv[rows_k]) + fix[1][rows_k]
            buf[1, z, at, :] = across * mh[pl.ds(r, 8), :] + along + wallward
        return 0

    def send(c):
        planes = pl.ds(c * per, per)
        return pltpu.make_async_copy(buf.at[:, planes], out.at[:, planes], sems.at[c])

    def group(g, _):
        lax.fori_loop(per * g, per * g + per, plane, 0)
        send(g).start()
        return 0

    lax.fori_loop(0, chunks, group, 0)
    for c in range(chunks):
        send(c).wait()


def call(body, name, inputs, specs, outputs, scratch, flops, moved, limit):
    return pl.pallas_call(
        body,
        name=name,
        in_specs=specs,
        out_specs=tuple(ANY if isinstance(o, jax.ShapeDtypeStruct) else WHOLE for o in outputs),
        out_shape=tuple(outputs),
        scratch_shapes=scratch,
        cost_estimate=pl.CostEstimate(flops=flops, bytes_accessed=moved, transcendentals=0),
        compiler_params=pltpu.CompilerParams(vmem_limit_bytes=limit),
    )(*inputs)


def keep(value):
    return pltpu.with_memory_space_constraint(value, pltpu.VMEM)


def shards(velocity, stream_metric, wall_metric):
    _, nz, columns, rows_here = velocity.shape
    n_gy = lax.axis_size("gy")
    last = n_gy - 1
    padded = columns + 2 * EDGE
    rows = columns + EDGE
    metric = stream_metric.reshape(2, columns)
    wall = wall_metric.reshape(n_gy, rows_here)

    sent = jnp.concatenate([velocity[:, :, :EDGE], velocity[:, :, columns - EDGE :]], axis=2)
    xr = lax.ppermute(sent, "gx", [(0, 1), (1, 0)])

    volume = nz * columns * rows_here
    mib = 1 << 20
    pad, v0, strip_a, strip_b, sums, mh = call(
        lambda *refs: prepare(nz, *refs),
        "prepare",
        (velocity, xr, metric, wall),
        [ANY, ANY, WHOLE, WHOLE],
        [
            pltpu.VMEM((2, nz, padded, LANES), F32),
            pltpu.VMEM((nz, padded, LANES), F32),
            pltpu.VMEM((9 * nz, LANES), F32),
            pltpu.VMEM((9 * nz, LANES), F32),
            pltpu.VMEM((rows, LANES), F32),
            pltpu.VMEM((padded, LANES), F32),
        ],
        [
            pltpu.VMEM((padded, LANES), F32),
            pltpu.VMEM((rows, LANES), F32),
            pltpu.VMEM((24, LANES), F32),
            pltpu.SemaphoreType.DMA((10,)),
        ],
        30 * volume,
        8 * volume,
        8 * mib,
    )
    pad, v0, mh = keep(pad), keep(v0), keep(mh)

    part, gxs = call(
        lambda *refs: stream_terms(nz, *refs),
        "stream_terms",
        (pad, mh),
        [WHOLE] * 2,
        [pltpu.VMEM((2, nz, columns, LANES), F32), pltpu.VMEM((3, nz, padded, LANES), F32)],
        [],
        40 * volume,
        8 * volume,
        4 * mib,
    )
    part, gxs = keep(part), keep(gxs)
    (dwall,) = call(
        lambda *refs: wall_terms(nz, last, *refs),
        "wall_terms",
        (pad, wall),
        [WHOLE] * 2,
        [pltpu.VMEM((2, nz, columns, LANES), F32)],
        [],
        40 * volume,
        8 * volume,
        4 * mib,
    )
    dwall = keep(dwall)
    part, gzs = call(
        lambda *refs: span_terms(nz, *refs),
        "span_terms",
        (pad, part),
        [WHOLE] * 2,
        [pltpu.VMEM((2, nz, columns, LANES), F32), pltpu.VMEM((3, nz, columns, LANES), F32)],
        [],
        40 * volume,
        8 * volume,
        4 * mib,
    )
    part, gzs = keep(part), keep(gzs)

    place = lax.axis_index("gy")
    pairs = [(i, i ^ 1) for i in range(n_gy)]
    others = [(i, i + 1) if i % 2 else (i, i - 1) for i in range(1, last)]
    total, below = sums, jnp.zeros_like(sums)
    got_a = lax.ppermute(strip_a, "gy", pairs)
    got_b = lax.ppermute(strip_b, "gy", others)
    hop = 1
    while hop < n_gy:
        came = lax.ppermute(total, "gy", [(i, i ^ hop) for i in range(n_gy)])
        below = below + jnp.where((place & hop) != 0, came, 0.0)
        total = total + came
        hop *= 2

    (out,) = call(
        lambda *refs: finish(nz, last, *refs),
        "finish",
        (pad, v0, part, dwall, gxs, gzs, mh, wall, strip_a, strip_b, got_a, got_b, below, total, sums),
        [WHOLE] * 15,
        [jax.ShapeDtypeStruct((3, nz, columns, rows_here), F32)],
        [
            pltpu.VMEM((nz, padded, LANES), F32),
            pltpu.VMEM((3, nz, columns, LANES), F32),
            pltpu.VMEM((24 * nz, LANES), F32),
            pltpu.VMEM((rows, 2 * LANES), BF16),
            pltpu.SemaphoreType.DMA((8,)),
        ],
        80 * volume,
        20 * volume,
        16 * mib,
    )
    return out


def solution(mesh):
    in_specs = (P(None, None, "gx", "gy"), P(), P())
    out_specs = P(None, None, "gx", "gy")
    return jax.shard_map(shards, mesh=mesh, in_specs=in_specs, out_specs=out_specs, check_vma=False)
```

time: 374 us -> 70.5 us (0.19)
  other arithmetic: 153 us -> 0.11 us
  blocking collectives: 106 us -> 0 us
  local copies, waits for them, and re-layouts: 93.3 us -> 9.16 us
  Pallas kernels: 0 us -> 37.5 us
  waiting for transfers between devices: 0.02 us -> 11.7 us
  starting transfers between devices: 16.6 us -> 11.5 us
    another operation x7 -> x0, other arithmetic: 115 us -> none  [the longest x4 115 us: shards(): return jnp.stack(outputs)]
    psum x1 -> x0, blocking collectives: 71.7 us -> none  [from_root(): return lax.psum(kept, axis)]
    slice x31 -> x1, local copies, waits for them, and re-layouts: 61.3 us -> 1.08 us  [shards(): velocity[:, :, :EDGE]]
    pallas_call x0 -> x5, Pallas kernels: none -> 37.5 us  [call(): pl.pallas_call(body, name=name, in_specs=specs, out_specs=tuple((ANY if i...]
    all_gather x1 -> x0, blocking collectives: 34.8 us -> none  [carried_in(): gathered = lax.all_gather(part, axis)]
    mul x3 -> x0, other arithmetic: 18.5 us -> none  [the longest x1 8.43 us: shards(): streamwise_wide * field_wide]
    ppermute x8 -> x7, waiting for transfers between devices: 0.02 us -> 11.7 us  [the longest x4 9.81 us: shards(): came = lax.ppermute(total, 'gy', [(i, i ^ hop) for i in range(n_gy)])]
    ppermute x4 -> x0, local copies, waits for them, and re-layouts: 10.8 us -> none  [the longest x2 5.45 us: padded(): after = lax.ppermute(first, axis, down)]
  transfers between devices with their start and end apart: 8 -> 7, of which waited for: 0 -> 4; matrix products, arithmetic and copies ran while one was open for 31% -> 0% of each run, Pallas kernels for 0% -> 19%
where the time goes in v1:
time: 70.5 us; the launch traced here: 70.1 us
  Pallas kernels  37.5 us (53%)
  waiting for transfers between devices  11.7 us (17%)
  starting transfers between devices  11.5 us (16%)
  local copies, waits for them, and re-layouts  9.16 us (13%)
    pallas_call x5, Pallas kernels, call(): pl.pallas_call(body, name=name, in_specs=specs, out_specs=tuple((ANY if i...  37.5 us
    ppermute x4, waiting for transfers between devices, shards(): came = lax.ppermute(total, 'gy', [(i, i ^ hop) for i in range(n_gy)])  9.81 us
    unnamed x14, local copies, waits for them, and re-layouts  8.08 us
    ppermute x4, starting transfers between devices, shards(): came = lax.ppermute(total, 'gy', [(i, i ^ hop) for i in range(n_gy)])  5.91 us
    ppermute x1, starting transfers between devices, shards(): got_b = lax.ppermute(strip_b, 'gy', others)  4.01 us
    ppermute x1, waiting for transfers between devices, shards(): xr = lax.ppermute(sent, 'gx', [(0, 1), (1, 0)])  1.9 us
    ppermute x1, starting transfers between devices, shards(): got_a = lax.ppermute(strip_a, 'gy', pairs)  1.49 us
  transfers between devices with their start and end apart: 7, of which 4 were waited for; matrix products, arithmetic and copies ran while one was open for 0% of the time, Pallas kernels for 19%

profile of v1, /device:TPU:8, one launch (start us, length us, event | category | flops | bytes accessed | tf_op | source)
XLA Modules:
  0.0 70.1 jit_solution(17940179113843359496)
XLA Ops:
  0.0 0.0 copy-start.5
  0.0 1.1 %fusion = (f32[2,32,8,128]{3,2,1,0:T(8,128)S(1)}, f32[2,32,8,128]{3,2,1,0:T(8,128)S(1)}) fusion(f32[2,32,128,128]{3,2,1,0:T(8,128)} %refs_0_.1), kind=kLoop, calls=%fused_computation.2 | loop fusion | bytes 1048576 | tf_op jit(solution)/shard_map/slice | solution.py:430
  1.1 0.1 collective-permute-start
  1.2 1.9 %collective-permute-done.refs_1_ = f32[2,32,16,128]{3,2,1,0:T(8,128)S(1)} collective-permute-done((f32[2,32,16,128]{3,2,1,0:T(8,128)S(1)}, f32[2,32,16,128]{3,2,1,0:T(8,128)S(1)}, u32[]{:S(2)}, u32[]{:S(2)}) %collective-permute-start) | collective-permute-done | bytes 524320 | tf_op jit(solution)/shard_map/ppermute | solution.py:431
  3.1 0.0 copy-start.3
  3.1 2.2 %copy-done.3 = f32[2,32,128,128]{3,2,1,0:T(8,128)S(1)} copy-done((f32[2,32,128,128]{3,2,1,0:T(8,128)S(1)}, f32[2,32,128,128]{3,2,1,0:T(8,128)}, u32[]{:S(2)}) %copy-start.3) | copy-done | bytes 4194328
  5.3 0.0 copy-start.4
  5.3 0.7 copy-done.4
  6.0 0.0 copy-start.6
  6.0 0.7 copy-done.6
  6.7 7.4 %prepare.1 = (f32[2,32,144,128]{3,2,1,0:T(8,128)S(1)}, f32[32,144,128]{2,1,0:T(8,128)S(1)}, f32[288,128]{1,0:T(8,128)S(1)}, f32[288,128]{1,0:T(8,128)S(1)}, f32[...) custom-call(f32[2,32,128,128]{3,2,1,0:T(8,128)S(1)} %copy-done.3, f32[2,32,16,128]{3,2,1,0:T(8,128)S(1)} %collective-permute-done.refs_1_, ...), custom_call_target="tpu_custom_call" | custom-call | flops 15728640 | bytes 4194304 | tf_op jit(solution)/shard_map/prepare/pallas_call | solution.py:405
  14.1 0.0 copy-start
  14.1 2.2 %copy-done = f32[2,32,144,128]{3,2,1,0:T(8,128)} copy-done((f32[2,32,144,128]{3,2,1,0:T(8,128)}, f32[2,32,144,128]{3,2,1,0:T(8,128)S(1)}, u32[]{:S(2)}) %copy-start) | copy-done | bytes 4718616
  16.2 1.5 %collective-permute-start.3 = (f32[136,128]{1,0:T(8,128)S(1)}, f32[136,128]{1,0:T(8,128)S(1)}, u32[]{:S(2)}, u32[]{:S(2)}) collective-permute-start(f32[136,128]{1,0:T(8,128)S(1)} %get-tuple-element.24.refs_14_), channel_id=1, source_target_pairs={{0,1},{1,0},{2,3},{3,2},{4,5},{5,4},{6,7},{7,6},{8,9},{9,8},{10,11... | collective-permute-start | bytes 208904 | tf_op jit(solution)/shard_map/ppermute | solution.py:505
  17.7 2.8 %collective-permute-done.3 = f32[136,128]{1,0:T(8,128)S(1)} collective-permute-done((f32[136,128]{1,0:T(8,128)S(1)}, f32[136,128]{1,0:T(8,128)S(1)}, u32[]{:S(2)}, u32[]{:S(2)}) %collective-permute-start.3) | collective-permute-done | bytes 69664 | tf_op jit(solution)/shard_map/ppermute | solution.py:505
  20.6 1.6 %collective-permute-start.4 = (f32[136,128]{1,0:T(8,128)S(1)}, f32[136,128]{1,0:T(8,128)S(1)}, u32[]{:S(2)}, u32[]{:S(2)}) collective-permute-start(f32[136,128]{1,0:T(8,128)S(1)} %add.21), channel_id=1, source_target_pairs={{0,2},{1,3},{2,0},{3,1},{4,6},{5,7},{6,4},{7,5},{8,10},{9,11},{10,... | collective-permute-start | bytes 208904 | tf_op jit(solution)/shard_map/ppermute | solution.py:505
  22.2 2.8 %collective-permute-done.4 = f32[136,128]{1,0:T(8,128)S(1)} collective-permute-done((f32[136,128]{1,0:T(8,128)S(1)}, f32[136,128]{1,0:T(8,128)S(1)}, u32[]{:S(2)}, u32[]{:S(2)}) %collective-permute-start.4) | collective-permute-done | bytes 69664 | tf_op jit(solution)/shard_map/ppermute | solution.py:505
  25.0 0.2 collective-permute-start.5
  25.1 4.2 %collective-permute-done.5 = f32[136,128]{1,0:T(8,128)S(1)} collective-permute-done((f32[136,128]{1,0:T(8,128)S(1)}, f32[136,128]{1,0:T(8,128)S(1)}, u32[]{:S(2)}, u32[]{:S(2)}) %collective-permute-start.5) | collective-permute-done | bytes 69664 | tf_op jit(solution)/shard_map/ppermute | solution.py:505
  29.3 2.7 %collective-permute-start.6 = (f32[136,128]{1,0:T(8,128)S(1)}, f32[136,128]{1,0:T(8,128)S(1)}, u32[]{:S(2)}, u32[]{:S(2)}) collective-permute-start(f32[136,128]{1,0:T(8,128)S(1)} %add.25), channel_id=1, source_target_pairs={{0,8},{1,9},{2,10},{3,11},{4,12},{5,13},{6,14},{7,15},{8,0},{9,1},... | collective-permute-start | bytes 208904 | tf_op jit(solution)/shard_map/ppermute | solution.py:505
  32.0 1.5 %collective-permute-start.1 = (f32[288,128]{1,0:T(8,128)S(1)}, f32[288,128]{1,0:T(8,128)S(1)}, u32[]{:S(2)}, u32[]{:S(2)}) collective-permute-start(f32[288,128]{1,0:T(8,128)S(1)} %get-tuple-element.22.refs_8_), channel_id=1, source_target_pairs={{0,1},{1,0},{2,3},{3,2},{4,5},{5,4},{6,7},{7,6},{8,9},{9,8},{10,11... | collective-permute-start | bytes 442376 | tf_op jit(solution)/shard_map/ppermute | solution.py:501
  33.5 4.0 %collective-permute-start.2 = (f32[288,128]{1,0:T(8,128)S(1)}, f32[288,128]{1,0:T(8,128)S(1)}, u32[]{:S(2)}, u32[]{:S(2)}) collective-permute-start(f32[288,128]{1,0:T(8,128)S(1)} %get-tuple-element.23.refs_9_), channel_id=1, source_target_pairs={{1,2},{2,1},{3,4},{4,3},{5,6},{6,5},{7,8},{8,7},{9,10},{10,9},{11,... | collective-permute-start | bytes 442376 | tf_op jit(solution)/shard_map/ppermute | solution.py:502
  37.5 0.0 copy-done.5
  37.5 0.0 copy-start.1
  37.5 2.3 %copy-done.1 = f32[2,32,144,128]{3,2,1,0:T(8,128)S(1)} copy-done((f32[2,32,144,128]{3,2,1,0:T(8,128)S(1)}, f32[2,32,144,128]{3,2,1,0:T(8,128)}, u32[]{:S(2)}) %copy-start.1) | copy-done | bytes 4718616
  39.9 0.0 copy-start.2
  39.9 5.8 %wall_terms.1.refs_3_ = f32[2,32,128,128]{3,2,1,0:T(8,128)S(1)} custom-call(f32[2,32,144,128]{3,2,1,0:T(8,128)S(1)} %copy-done.1, f32[16,128]{1,0:T(8,128)S(1)} %bitcast.3), custom_call_target="tpu_custom_call" | custom-call | flops 20971520 | bytes 4194304 | tf_op jit(solution)/shard_map/wall_terms/pallas_call | solution.py:405
  45.6 0.0 copy-done.2
  45.6 3.2 %stream_terms.1 = (f32[2,32,128,128]{3,2,1,0:T(8,128)S(1)}, f32[3,32,144,128]{3,2,1,0:T(8,128)S(1)}) custom-call(f32[2,32,144,128]{3,2,1,0:T(8,128)S(1)} %copy-done.2, f32[144,128]{1,0:T(8,128)S(1)} %get-tuple-element.17.refs_1_.refs_6_), custom_call_target="tpu_custom_call" | custom-call | flops 20971520 | bytes 4194304 | tf_op jit(solution)/shard_map/stream_terms/pallas_call | solution.py:405
  48.9 4.0 %span_terms.1 = (f32[2,32,128,128]{3,2,1,0:T(8,128)S(1)}, f32[3,32,128,128]{3,2,1,0:T(8,128)S(1)}) custom-call(f32[2,32,144,128]{3,2,1,0:T(8,128)S(1)} %copy-done.2, f32[2,32,128,128]{3,2,1,0:T(8,128)S(1)} %get-tuple-element.18.refs_1_), custom_call_target="tpu_custom_call" | custom-call | flops 20971520 | bytes 4194304 | tf_op jit(solution)/shard_map/span_terms/pallas_call | solution.py:405
  52.9 0.0 collective-permute-done.6
  53.0 0.0 collective-permute-done.1.refs_10_
  53.0 0.0 collective-permute-done.2.refs_11_
  53.0 17.1 %finish.1 = f32[3,32,128,128]{3,2,1,0:T(8,128)} custom-call(f32[2,32,144,128]{3,2,1,0:T(8,128)S(1)} %copy-done.2, f32[32,144,128]{2,1,0:T(8,128)S(1)} %get-tuple-element.16.refs_1_, f32[2,32,128,128]{3,2,1,0:T(8,128)S(1)} %get-tuple-element.19.refs_2_, f32[2,32,128,128]{3,2,1,0:T(8,128)S(1)} %wall_terms.1.refs_3_, ...), custom_call_target="tpu_custom_call" | custom-call | flops 41943040 | bytes 10485760 | tf_op jit(solution)/shard_map/finish/pallas_call | solution.py:405
  (5 shorter events, 0.1 us)
Async XLA Ops:
  0.0 37.5 %copy-start.5 = (f32[2048]{0:T(1024)S(1)}, f32[2048]{0:T(1024)}, u32[]{:S(2)}) copy-start(f32[2048]{0:T(1024)} %param.5) | copy-start | bytes 24580
  1.1 2.0 %collective-permute-start = (f32[2,32,16,128]{3,2,1,0:T(8,128)S(1)}, f32[2,32,16,128]{3,2,1,0:T(8,128)S(1)}, u32[]{:S(2)}, u32[]{:S(2)}) collective-permute-start(f32[2,32,16,128]{3,2,1,0:T(8,128)S(1)} %pad_maximum_fusion), channel_id=1, source_target_pairs={{0,16},{16,0},{1,17},{17,1},{2,18},{18,2},{3,19},{19,3},{4,20},{20... | collective-permute-start | bytes 1572872 | tf_op jit(solution)/shard_map/ppermute | solution.py:431
  3.1 2.2 %copy-start.3 = (f32[2,32,128,128]{3,2,1,0:T(8,128)S(1)}, f32[2,32,128,128]{3,2,1,0:T(8,128)}, u32[]{:S(2)}) copy-start(f32[2,32,128,128]{3,2,1,0:T(8,128)} %refs_0_.1) | copy-start | bytes 12582916
  5.3 0.7 copy-start.4
  6.0 0.7 copy-start.6
  14.1 2.2 %copy-start = (f32[2,32,144,128]{3,2,1,0:T(8,128)}, f32[2,32,144,128]{3,2,1,0:T(8,128)S(1)}, u32[]{:S(2)}) copy-start(f32[2,32,144,128]{3,2,1,0:T(8,128)S(1)} %get-tuple-element.15.refs_0_) | copy-start | bytes 14155780
  16.2 4.3 %collective-permute-start.3 = (f32[136,128]{1,0:T(8,128)S(1)}, f32[136,128]{1,0:T(8,128)S(1)}, u32[]{:S(2)}, u32[]{:S(2)}) collective-permute-start(f32[136,128]{1,0:T(8,128)S(1)} %get-tuple-element.24.refs_14_), channel_id=1, source_target_pairs={{0,1},{1,0},{2,3},{3,2},{4,5},{5,4},{6,7},{7,6},{8,9},{9,8},{10,11... | collective-permute-start | bytes 208904 | tf_op jit(solution)/shard_map/ppermute | solution.py:505
  20.6 4.4 %collective-permute-start.4 = (f32[136,128]{1,0:T(8,128)S(1)}, f32[136,128]{1,0:T(8,128)S(1)}, u32[]{:S(2)}, u32[]{:S(2)}) collective-permute-start(f32[136,128]{1,0:T(8,128)S(1)} %add.21), channel_id=1, source_target_pairs={{0,2},{1,3},{2,0},{3,1},{4,6},{5,7},{6,4},{7,5},{8,10},{9,11},{10,... | collective-permute-start | bytes 208904 | tf_op jit(solution)/shard_map/ppermute | solution.py:505
  25.0 4.4 %collective-permute-start.5 = (f32[136,128]{1,0:T(8,128)S(1)}, f32[136,128]{1,0:T(8,128)S(1)}, u32[]{:S(2)}, u32[]{:S(2)}) collective-permute-start(f32[136,128]{1,0:T(8,128)S(1)} %add.23), channel_id=1, source_target_pairs={{0,4},{1,5},{2,6},{3,7},{4,0},{5,1},{6,2},{7,3},{8,12},{9,13},{10,... | collective-permute-start | bytes 208904 | tf_op jit(solution)/shard_map/ppermute | solution.py:505
  29.3 23.6 %collective-permute-start.6 = (f32[136,128]{1,0:T(8,128)S(1)}, f32[136,128]{1,0:T(8,128)S(1)}, u32[]{:S(2)}, u32[]{:S(2)}) collective-permute-start(f32[136,128]{1,0:T(8,128)S(1)} %add.25), channel_id=1, source_target_pairs={{0,8},{1,9},{2,10},{3,11},{4,12},{5,13},{6,14},{7,15},{8,0},{9,1},... | collective-permute-start | bytes 208904 | tf_op jit(solution)/shard_map/ppermute | solution.py:505
  32.0 21.0 %collective-permute-start.1 = (f32[288,128]{1,0:T(8,128)S(1)}, f32[288,128]{1,0:T(8,128)S(1)}, u32[]{:S(2)}, u32[]{:S(2)}) collective-permute-start(f32[288,128]{1,0:T(8,128)S(1)} %get-tuple-element.22.refs_8_), channel_id=1, source_target_pairs={{0,1},{1,0},{2,3},{3,2},{4,5},{5,4},{6,7},{7,6},{8,9},{9,8},{10,11... | collective-permute-start | bytes 442376 | tf_op jit(solution)/shard_map/ppermute | solution.py:501
  33.5 19.5 %collective-permute-start.2 = (f32[288,128]{1,0:T(8,128)S(1)}, f32[288,128]{1,0:T(8,128)S(1)}, u32[]{:S(2)}, u32[]{:S(2)}) collective-permute-start(f32[288,128]{1,0:T(8,128)S(1)} %get-tuple-element.23.refs_9_), channel_id=1, source_target_pairs={{1,2},{2,1},{3,4},{4,3},{5,6},{6,5},{7,8},{8,7},{9,10},{10,9},{11,... | collective-permute-start | bytes 442376 | tf_op jit(solution)/shard_map/ppermute | solution.py:502
  37.5 2.3 %copy-start.1 = (f32[2,32,144,128]{3,2,1,0:T(8,128)S(1)}, f32[2,32,144,128]{3,2,1,0:T(8,128)}, u32[]{:S(2)}) copy-start(f32[2,32,144,128]{3,2,1,0:T(8,128)} %copy-done) | copy-start | bytes 14155780
  39.9 5.8 %copy-start.2 = (f32[2,32,144,128]{3,2,1,0:T(8,128)S(1)}, f32[2,32,144,128]{3,2,1,0:T(8,128)}, u32[]{:S(2)}) copy-start(f32[2,32,144,128]{3,2,1,0:T(8,128)} %copy-done) | copy-start | bytes 14155780

commit v2 on v1

v2 whole, which is shorter than its diff:
```python
import jax
import jax.numpy as jnp
from jax import lax
from jax.experimental import pallas as pl
from jax.experimental.pallas import tpu as pltpu
from jax.sharding import PartitionSpec as P

F32 = jnp.float32
BF16 = jnp.bfloat16
HALF60 = 0.5 / 60.0
CENTRAL = ((1, 45.0), (2, -9.0), (3, 1.0))
WALL_ROWS = (
    {0: -110.0, 1: 180.0, 2: -90.0, 3: 20.0},
    {-1: -20.0, 0: -30.0, 1: 60.0, 2: -10.0},
    {-2: 5.0, -1: -40.0, 1: 40.0, 2: -5.0},
)
LANES = 128
GROUP = 4
EDGE = 8
LOW = EDGE - 3

WHOLE = pl.BlockSpec(memory_space=pltpu.VMEM)
HBM = pl.BlockSpec(memory_space=pltpu.HBM)


def iota(shape, dim):
    return lax.broadcasted_iota(jnp.int32, shape, dim)


def split(value):
    high = value.astype(BF16)
    low = (value - high.astype(F32)).astype(BF16)
    return jnp.concatenate([high, low], axis=1)


def wrapped(plane, nz):
    return lax.rem(plane + nz, nz)


def wall_matrix(place, last):
    h = iota((LANES, LANES), 0)
    j = iota((LANES, LANES), 1)
    away = h - j
    inner = jnp.zeros((LANES, LANES), F32)
    for distance, weight in CENTRAL:
        inner = jnp.where(away == distance, weight, inner)
        inner = jnp.where(away == -distance, -weight, inner)
    for row, entries in enumerate(WALL_ROWS):
        for side in (0, 1):
            at = row if side == 0 else LANES - 1 - row
            sign = 1 if side == 0 else -1
            closed = jnp.zeros((LANES, LANES), F32)
            for offset, weight in entries.items():
                closed = jnp.where(away == sign * offset, sign * weight, closed)
            here = jnp.where(place == (0 if side == 0 else last), 1, 0)
            inner = jnp.where((j == at) & (here == 1), closed, inner)
    inner = inner.astype(BF16)
    return jnp.concatenate([inner, inner], axis=0)


def heights(wall, block, blocks):
    cell = 1.0 / wall[...]
    row = iota(cell.shape, 0)
    total = jnp.sum(cell)
    before = jnp.sum(jnp.where(row < block, cell, 0.0))
    mine = 1.0 / wall[pl.ds(block, 1), :]
    prefix = mine
    lane = iota((1, LANES), 1)
    for shift in (1, 2, 4, 8, 16, 32, 64):
        prefix = prefix + jnp.where(lane >= shift, pltpu.roll(prefix, shift, 1), 0.0)
    return (before + prefix - 0.5 * mine) / total


def sum_rows(nz, last, vel, metric_hbm, wall_hbm, pad, uw, ms, mh, vectors, matrix, bits, masks, metric, wall, sems):
    gx = lax.axis_index("gx")
    gy = lax.axis_index("gy")
    columns = uw.shape[0]
    chunks = 8
    per = nz // chunks

    def chunk(c):
        planes = pl.ds(c * per, per)
        return pltpu.make_async_copy(vel.at[:, planes], pad.at[:, planes, pl.ds(EDGE, columns)], sems.at[c])

    small = [
        pltpu.make_async_copy(wall_hbm, wall, sems.at[chunks]),
        pltpu.make_async_copy(metric_hbm, metric, sems.at[chunks + 1]),
    ]
    for copy in small:
        copy.start()
    for c in range(chunks):
        chunk(c).start()
    matrix[...] = wall_matrix(gy, last)
    plane = iota(masks.shape, 0) // 8
    masks[...] = jnp.where(lax.rem(iota(masks.shape, 1), nz) == plane, 1.0, 0.0).astype(BF16)
    for copy in small:
        copy.wait()
    own = jnp.broadcast_to(metric[pl.ds(gx, 1), :], (LANES, columns)).T
    peer = jnp.broadcast_to(metric[pl.ds(1 - gx, 1), :], (LANES, columns)).T
    ms[0:EDGE, :] = peer[columns - EDGE :]
    ms[EDGE : EDGE + columns, :] = own
    ms[EDGE + columns :, :] = peer[:EDGE]
    mh[...] = ms[...] * HALF60
    wall_here = wall[pl.ds(gy, 1), :]
    rw = 1.0 / wall_here
    vectors[0:1, :] = heights(wall, jnp.maximum(gy - 1, 0), last + 1)
    vectors[1:2, :] = heights(wall, gy, last + 1)
    vectors[2:3, :] = heights(wall, jnp.minimum(gy + 1, last), last + 1)
    vectors[3:4, :] = wall_here * HALF60
    vectors[4:5, :] = rw
    vectors[5:8, :] = jnp.zeros((3, LANES), F32)
    for i in range(bits.shape[0]):
        bits[i : i + 1, :] = jnp.full((1, LANES), jnp.where((gy & (1 << i)) != 0, 1.0, 0.0), F32)
    lane = iota((columns, LANES), 1)

    def group(g, held):
        chunk(g).wait()
        for p in range(per):
            z = g * per + p
            for c in range(2):
                line = jnp.sum(pad[c, z, pl.ds(EDGE, columns), :] * rw, axis=1, keepdims=True)
                held = jnp.where(lane == z + c * nz, line, held)
        return held

    uw[...] = lax.fori_loop(0, chunks, group, jnp.zeros((columns, LANES), F32))


def sum_slopes(nz, xr, uw, ms, vectors, sums, wide):
    columns = uw.shape[0]
    rows = columns + EDGE
    rw = vectors[4:5, :]
    lane = iota((2 * EDGE, LANES), 1)
    held = jnp.zeros((2 * EDGE, LANES), F32)
    for z in range(nz):
        for c in range(2):
            line = jnp.sum(xr[c, z] * rw, axis=1, keepdims=True)
            held = jnp.where(lane == z + c * nz, line, held)
    wide[0:EDGE, :] = held[EDGE:]
    wide[EDGE : EDGE + columns, :] = uw[...]
    wide[EDGE + columns :, :] = held[:EDGE]
    centre = wide[pl.ds(LOW, rows), :]
    lane = iota((rows, LANES), 1)
    around = jnp.where(lane < nz, pltpu.roll(centre, LANES - nz, 1), centre)
    around = jnp.where(lane < 2 * nz, around, pltpu.roll(around, 2 * nz, 1))
    du = dw = None
    for distance, weight in CENTRAL:
        a = weight * (wide[pl.ds(LOW + distance, rows), :] - wide[pl.ds(LOW - distance, rows), :])
        b = weight * (pltpu.roll(around, LANES - distance, 1) - pltpu.roll(around, distance, 1))
        du = a if du is None else du + a
        dw = b if dw is None else dw + b
    total = (ms[pl.ds(LOW, rows), :] * du + dw) * (1.0 / 60.0)
    sums[...] = jnp.where(lane < nz, total, 0.0)


def edge_columns(first_lane):
    h = iota((LANES, LANES), 0)
    lane = iota((LANES, LANES), 1) - first_lane
    last = (lane >= 0) & (lane < 3) & (h == lane + LANES - 3)
    first = (lane >= 3) & (lane < 6) & (h == lane - 3)
    picked = jnp.where(last | first, 1.0, 0.0).astype(BF16)
    return jnp.concatenate([picked, picked], axis=0)


def prepare(
    nz, pad_in, xr, ms, vectors, matrix, pad, v0, dwall, strip_a, strip_b, token,
    weights_s, weights_u, weights_w, halves_s, halves_u, halves_w, edges, turned,
):
    del pad_in
    gy = lax.axis_index("gy")
    columns = dwall.shape[2]
    rows = columns + EDGE
    tall = rows // 8
    rw60 = vectors[4:5, :] * (1.0 / 60.0)
    scale = vectors[3:4, :]
    h = iota((LANES, LANES), 0)
    j = iota((LANES, LANES), 1)
    climb = jnp.where(h < j, -1.0, jnp.where(h == j, -0.5, 0.0)).astype(BF16)
    weights_s[:, :LANES] = jnp.concatenate([climb, climb], axis=0)
    weights_s[:, LANES:] = edge_columns(12)
    weights_u[:, :LANES] = matrix[...]
    weights_u[:, LANES:] = edge_columns(0)
    weights_w[:, :LANES] = matrix[...]
    weights_w[:, LANES:] = edge_columns(6)
    odd = lax.rem(gy, 2) == 1
    token[...] = jnp.zeros(token.shape, F32)
    pad[:, :, pl.ds(0, EDGE), :] = xr[:, :, pl.ds(EDGE, EDGE), :]
    pad[:, :, pl.ds(EDGE + columns, EDGE), :] = xr[:, :, pl.ds(0, EDGE), :]

    def gather(g):
        blocks = []
        for p in range(GROUP):
            z = g * GROUP + p
            ups = [wrapped(z + d, nz) for d in (1, 2, 3)]
            downs = [wrapped(z - d, nz) for d in (1, 2, 3)]
            for k in range(tall):
                r = LOW + 8 * k
                du = dw = None
                for distance, weight in CENTRAL:
                    a = pad[0, z, pl.ds(r + distance, 8), :] - pad[0, z, pl.ds(r - distance, 8), :]
                    b = pad[1, ups[distance - 1], pl.ds(r, 8), :] - pad[1, downs[distance - 1], pl.ds(r, 8), :]
                    if weight != 1.0:
                        a, b = weight * a, weight * b
                    du = a if du is None else du + a
                    dw = b if dw is None else dw + b
                blocks.append((ms[pl.ds(r, 8), :] * du + dw) * rw60)
                if len(blocks) == 2:
                    halves_s[pl.ds(8 * (p * tall + k - 1), 16), :] = split(jnp.concatenate(blocks, axis=0))
                    blocks = []
            halves_u[pl.ds(p * columns, columns), :] = split(pad[0, z, pl.ds(EDGE, columns), :])
            halves_w[pl.ds(p * columns, columns), :] = split(pad[1, z, pl.ds(EDGE, columns), :])

    def settle(g):
        made_s = jnp.dot(halves_s[...], weights_s[...], preferred_element_type=F32)
        for p in range(GROUP):
            here = made_s[p * rows : (p + 1) * rows]
            v0[g * GROUP + p, pl.ds(LOW, rows), :] = here[:, :LANES]
            edges[p] = here[:, LANES:]
        made_u = jnp.dot(halves_u[...], weights_u[...], preferred_element_type=F32)
        made_w = jnp.dot(halves_w[...], weights_w[...], preferred_element_type=F32)
        for p in range(GROUP):
            z = g * GROUP + p
            at = slice(p * columns, (p + 1) * columns)
            dwall[0, z] = made_u[at, :LANES] * scale
            dwall[1, z] = made_w[at, :LANES] * scale
            packed = made_u[at, LANES:] + made_w[at, LANES:] + edges[p, pl.ds(3, columns), :]
            turned[p] = packed.T[:24]
            for f in range(3):
                last = turned[p, 6 * f : 6 * f + 3, :]
                first = turned[p, 6 * f + 3 : 6 * f + 6, :]
                strip_a[pl.ds(3 * f * nz + z, 3, stride=nz), :] = jnp.where(odd, first, last)
                strip_b[pl.ds(3 * f * nz + z, 3, stride=nz), :] = jnp.where(odd, last, first)

    def step(g, _):
        settle(g)
        gather(g + 1)
        return 0

    groups = nz // GROUP
    gather(0)
    lax.fori_loop(0, groups - 1, step, 0)
    settle(groups - 1)


def known_terms(nz, pad, mh, wait_a, wait_b, pad_out, part, gx_out, gz_out, token):
    del pad_out, wait_a, wait_b
    columns = part.shape[2]
    token[...] = jnp.zeros(token.shape, F32)
    for z in range(nz):
        u = pad[0, z, pl.ds(0, 8), :]
        for distance, weight in CENTRAL:
            gx_out[distance - 1, z, pl.ds(0, 8), :] = weight * (u + pad[0, z, pl.ds(distance, 8), :])

    def block(k, _):
        r = pl.multiple_of(8 * k + EDGE, 8)
        at = pl.ds(pl.multiple_of(8 * k, 8), 8)
        metric = mh[pl.ds(r, 8), :]
        field = [{}, {}]
        factor = {}

        def load(c, z):
            if z not in field[c]:
                field[c][z] = pad[c, z % nz, pl.ds(r, 8), :]
            return field[c][z]

        def span_factor(distance, weight, z):
            if (distance, z) not in factor:
                factor[distance, z] = (load(1, z) + load(1, z + distance)) * (weight * HALF60)
            return factor[distance, z]

        for z in range(nz):
            u = load(0, z)
            across = [None, None]
            along = [None, None]
            for distance, weight in CENTRAL:
                ahead = [pad[c, z, pl.ds(r + distance, 8), :] for c in range(2)]
                behind = [pad[c, z, pl.ds(r - distance, 8), :] for c in range(2)]
                g, g_low = u + ahead[0], u + behind[0]
                if weight != 1.0:
                    g, g_low = weight * g, weight * g_low
                gx_out[distance - 1, z, pl.ds(r, 8), :] = g
                s = span_factor(distance, weight, z)
                s_low = span_factor(distance, weight, z - distance)
                gz_out[distance - 1, z, at, :] = s
                for c in range(2):
                    a = g * ahead[c] - g_low * behind[c]
                    b = s * load(c, z + distance) - s_low * load(c, z - distance)
                    across[c] = a if across[c] is None else across[c] + a
                    along[c] = b if along[c] is None else along[c] + b
            for c in range(2):
                part[c, z, at, :] = across[c] * metric + along[c]
        return 0

    lax.fori_loop(0, columns // 8, block, 0)


def finish(
    nz, last, pad, v0, part, dwall, gxs, gzs, mh, vectors, matrix, masks, own_a, own_b, got_a, got_b, below, total, sums,
    out, v, buf, fixes, lhs, halves, slopes, turned, sems,
):
    gy = lax.axis_index("gy")
    columns = buf.shape[2]
    rows = columns + EDGE
    odd = lax.rem(gy, 2) == 1
    frac_low, frac, frac_high, scale = (vectors[i : i + 1, :] for i in range(4))

    def strip(pick, f, r):
        at = pl.ds((3 * f + r) * nz, nz)
        return pick[0][at, :], pick[1][at, :]

    def own_first(f, r):
        a, b = strip((own_a, own_b), f, r)
        return jnp.where(odd, a, b)

    def own_last(f, r):
        a, b = strip((own_a, own_b), f, r)
        return jnp.where(odd, b, a)

    def from_low(f, r):
        a, b = strip((got_a, got_b), f, r)
        return jnp.where(odd, a, b)

    def from_high(f, r):
        a, b = strip((got_a, got_b), f, r)
        return jnp.where(odd, b, a)

    def compact(ref):
        return ref[pl.ds(3, columns), :].T[:nz]

    below_c = compact(below)
    total_c = compact(total)
    incl_c = below_c + compact(sums)
    lane_one = lambda vector, at: vector[:, at : at + 1]

    def climb(start, slopes, sign, fractions):
        level, made = start, []
        for slope, fraction in zip(slopes, fractions):
            made.append(fraction * total_c - (level + (0.5 * sign) * slope))
            level = level + sign * slope
        return made

    v_first = climb(below_c, [own_first(2, r) for r in range(3)], 1.0, [lane_one(frac, r) for r in range(3)])
    v_last = climb(incl_c, [own_last(2, 2 - q) for q in range(3)], -1.0, [lane_one(frac, LANES - 1 - q) for q in range(3)])
    v_low = climb(below_c, [from_low(2, 2 - q) for q in range(3)], -1.0, [lane_one(frac_low, LANES - 1 - q) for q in range(3)])
    v_high = climb(incl_c, [from_high(2, r) for r in range(3)], 1.0, [lane_one(frac_high, r) for r in range(3)])
    v_low = [jnp.where(gy > 0, x, 0.0) for x in v_low]
    v_high = [jnp.where(gy < last, x, 0.0) for x in v_high]
    weight_of = dict(CENTRAL)
    for i in (15, 16, 17, 18, 19, 20):
        fixes[pl.ds(i * nz, nz), :] = jnp.zeros((nz, LANES), F32)
    for c in range(3):
        for side in range(2):
            v_own, v_out = (v_first, v_low) if side == 0 else (v_last, v_high)
            for q in range(3):
                value = None
                for m in range(3 - q):
                    if c == 1:
                        field = v_out[m]
                    elif side == 0:
                        field = from_low(c // 2, 2 - m)
                    else:
                        field = from_high(c // 2, m)
                    weight = weight_of[q + m + 1] * (-1.0 if side == 0 else 1.0)
                    term = weight * ((v_own[q] + v_out[m]) * field)
                    value = term if value is None else value + term
                at = q if side == 0 else LANES - 1 - q
                if c == 0:
                    row = q if side == 0 else 23 - q
                else:
                    row = 6 * c - 3 + (3 + q if side == 0 else 2 - q)
                fixes[pl.ds(row * nz, nz), :] = value * lane_one(scale, at)

    below_v = below[...]
    total_v = total[...]
    below_h = below_v.astype(BF16).astype(F32)
    below_l = below_v - below_h
    total_h = total_v.astype(BF16).astype(F32)
    total_l = total_v - total_h
    quarter = iota((rows, LANES), 1) // nz
    first_half = jnp.where(
        quarter == 0,
        below_h,
        jnp.where(
            quarter == 1,
            pltpu.roll(below_l, nz, 1),
            jnp.where(quarter == 2, pltpu.roll(total_h, 2 * nz, 1), pltpu.roll(total_l, 3 * nz, 1)),
        ),
    )
    second_half = jnp.where(quarter == 0, total_h, jnp.where(quarter == 1, pltpu.roll(total_l, nz, 1), 0.0))
    both = jnp.concatenate([first_half, second_half], axis=1).astype(BF16).astype(F32)
    for k in range(rows // 8):
        block = both[8 * k : 8 * k + 8]
        lhs[pl.ds(16 * k, 16), :] = jnp.concatenate([block, block], axis=0).astype(BF16)
    frac_h = frac.astype(BF16).astype(F32)
    frac_l = frac - frac_h
    k_index = iota((2 * LANES, LANES), 0)
    base = jnp.where(
        k_index < 2 * nz,
        -1.0,
        jnp.where(k_index < LANES, jnp.broadcast_to(frac_h, (2 * LANES, LANES)), jnp.broadcast_to(frac_l, (2 * LANES, LANES))),
    ).astype(BF16)
    tall = rows // 8

    def make_v(g):
        chosen = []
        for pair in range(GROUP // 2):
            mask = masks[pl.ds(pl.multiple_of(8 * (g * GROUP + 2 * pair), 16), 16), :]
            chosen += [lhs[pl.ds(16 * k, 16), :] * mask for k in range(tall)]
        level = jnp.dot(jnp.concatenate(chosen, axis=0), base, preferred_element_type=F32)
        for p in range(GROUP):
            for k in range(tall):
                at = pl.ds(LOW + 8 * k, 8)
                row = 16 * (p // 2 * tall + k) + 8 * (p % 2)
                v[g * GROUP + p, at, :] = v0[g * GROUP + p, at, :] + level[row : row + 8]

    def make_halves(g):
        for p in range(GROUP):
            z = g * GROUP + p
            here = v[z, pl.ds(EDGE, columns), :]
            for i, factor in enumerate((None, here, pad[0, z, pl.ds(EDGE, columns), :], pad[1, z, pl.ds(EDGE, columns), :])):
                halves[pl.ds((4 * p + i) * columns, columns), :] = split(here if factor is None else here * factor)

    def make_slopes():
        slopes[...] = jnp.dot(halves[...], matrix[...], preferred_element_type=F32)

    zeros = jnp.zeros((LANES - 24, LANES), F32)

    def make_turned(g):
        for p in range(GROUP):
            z = g * GROUP + p
            low = fixes[pl.ds(z, 16, stride=nz), :]
            high = fixes[pl.ds(16 * nz + z, 8, stride=nz), :]
            turned[p] = jnp.concatenate([low, zeros, high], axis=0).T

    groups = nz // GROUP
    for g in (groups - 1, 0, 1, 2):
        make_v(g)
    make_halves(0)
    make_slopes()
    make_turned(0)
    make_halves(1)
    lane = iota((8, LANES), 1)
    at_edge = (lane < 3) | (lane >= LANES - 3)

    def complete(g):
        for k in range(columns // 8):
            r = EDGE + 8 * k
            at = pl.ds(8 * k, 8)
            metric = mh[pl.ds(r, 8), :]
            level, factor = {}, {}

            def v_at(g, p):
                if p not in level:
                    level[p] = v[wrapped(g * GROUP + p, nz), pl.ds(r, 8), :]
                return level[p]

            def span_factor(g, distance, p):
                if (distance, p) not in factor:
                    factor[distance, p] = gzs[distance - 1, wrapped(g * GROUP + p, nz), at, :]
                return factor[distance, p]

            for p in range(GROUP):
                z = g * GROUP + p
                here = v_at(g, p)
                edge = turned[p, at, :]
                fix = [edge, pltpu.roll(edge, LANES - 6, 1), pltpu.roll(edge, LANES - 12, 1)]
                fix = [jnp.where(at_edge, x, 0.0) for x in fix]
                d_v, d_vv, d_vu, d_vw = (slopes[pl.ds((4 * p + i) * columns + 8 * k, 8), :] for i in range(4))
                buf[0, z, at, :] = part[0, z, at, :] + here * dwall[0, z, at, :] + (scale * d_vu + fix[0])
                buf[2, z, at, :] = part[1, z, at, :] + here * dwall[1, z, at, :] + (scale * d_vw + fix[2])
                across = along = None
                for distance, _w in CENTRAL:
                    a = gxs[distance - 1, z, pl.ds(r, 8), :] * v[z, pl.ds(r + distance, 8), :]
                    a = a - gxs[distance - 1, z, pl.ds(r - distance, 8), :] * v[z, pl.ds(r - distance, 8), :]
                    b = span_factor(g, distance, p) * v_at(g, p + distance)
                    b = b - span_factor(g, distance, p - distance) * v_at(g, p - distance)
                    across = a if across is None else across + a
                    along = b if along is None else along + b
                wallward = scale * (here * d_v + d_vv) + fix[1]
                buf[1, z, at, :] = across * metric + along + wallward

    def send(g):
        planes = pl.ds(g * GROUP, GROUP)
        return pltpu.make_async_copy(buf.at[:, planes], out.at[:, planes], sems.at[g])

    def step(g, _):
        complete(g)
        make_slopes()
        make_turned(wrapped(g + 1, groups))
        make_halves(wrapped(g + 2, groups))
        make_v(wrapped(g + 3, groups))
        send(g).start()
        return 0

    lax.fori_loop(0, groups, step, 0)
    for g in range(groups):
        send(g).wait()


def call(body, name, inputs, outputs, scratch, flops, moved, limit, far=(), aliases=None):
    return pl.pallas_call(
        body,
        name=name,
        in_specs=[HBM if i in far else WHOLE for i in range(len(inputs))],
        out_specs=tuple(HBM if isinstance(o, jax.ShapeDtypeStruct) else WHOLE for o in outputs),
        out_shape=tuple(outputs),
        scratch_shapes=scratch,
        input_output_aliases=aliases or {},
        cost_estimate=pl.CostEstimate(flops=flops, bytes_accessed=moved, transcendentals=0),
        compiler_params=pltpu.CompilerParams(vmem_limit_bytes=limit),
    )(*inputs)


def keep(*values):
    return [pltpu.with_memory_space_constraint(value, pltpu.VMEM) for value in values]


def shards(velocity, stream_metric, wall_metric):
    _, nz, columns, rows_here = velocity.shape
    n_gy = lax.axis_size("gy")
    last = n_gy - 1
    padded = columns + 2 * EDGE
    rows = columns + EDGE
    metric = stream_metric.reshape(2, columns)
    wall = wall_metric.reshape(n_gy, rows_here)
    volume = nz * columns * rows_here
    mib = 1 << 20
    vmem = lambda *shape: pltpu.VMEM(shape, F32)
    pad_shape = vmem(2, nz, padded, LANES)
    token_shape = vmem(rows, LANES)

    sent = jnp.concatenate([velocity[:, :, :EDGE], velocity[:, :, columns - EDGE :]], axis=2)
    xr = lax.ppermute(sent, "gx", [(0, 1), (1, 0)])

    near = pltpu.with_memory_space_constraint(velocity, pltpu.HBM)
    metric = pltpu.with_memory_space_constraint(metric, pltpu.HBM)
    wall = pltpu.with_memory_space_constraint(wall, pltpu.HBM)
    pad, uw, ms, mh, vectors, matrix, bits, masks = call(
        lambda *refs: sum_rows(nz, last, *refs),
        "sum_rows",
        (near, metric, wall),
        [pad_shape, vmem(columns, LANES), vmem(padded, LANES), vmem(padded, LANES), vmem(8, LANES), pltpu.VMEM((2 * LANES, LANES), BF16), vmem(8, LANES), pltpu.VMEM((8 * nz, 2 * LANES), BF16)],
        [vmem(2, columns), vmem(n_gy, rows_here), pltpu.SemaphoreType.DMA((10,))],
        4 * volume,
        8 * volume,
        2 * mib,
        far=(0, 1, 2),
    )
    pad, uw, ms, mh, vectors, matrix, masks = keep(pad, uw, ms, mh, vectors, matrix, masks)
    (sums,) = call(
        lambda *refs: sum_slopes(nz, *refs),
        "sum_slopes",
        (xr, uw, ms, vectors),
        [vmem(rows, LANES)],
        [vmem(padded, LANES)],
        volume // 4,
        volume // 2,
        2 * mib,
    )

    def scan_step(level, total, below, token=None):
        came = lax.ppermute(total, "gy", [(i, i ^ (1 << level)) for i in range(n_gy)])
        below = below + came * bits[level : level + 1]
        total = total + came
        return (total if token is None else total + token), below, came

    half = lambda count: pltpu.VMEM((count, 2 * LANES), BF16)
    pad, v0, dwall, strip_a, strip_b, token = call(
        lambda *refs: prepare(nz, *refs),
        "prepare",
        (pad, xr, ms, vectors, matrix),
        [pad_shape, vmem(nz, padded, LANES), vmem(2, nz, columns, LANES), vmem(9 * nz, LANES), vmem(9 * nz, LANES), token_shape],
        [half(2 * LANES)] * 3
        + [half(GROUP * rows), half(GROUP * columns), half(GROUP * columns), vmem(GROUP, rows, LANES), vmem(GROUP, 24, LANES)],
        60 * volume,
        8 * volume,
        6 * mib,
        aliases={0: 0},
    )
    pad, v0, dwall = keep(pad, v0, dwall)
    total, below, came = scan_step(0, sums, jnp.zeros_like(sums), token)

    got_a = lax.ppermute(strip_a, "gy", [(i, i ^ 1) for i in range(n_gy)])
    got_b = lax.ppermute(strip_b, "gy", [(i, i + 1) if i % 2 else (i, i - 1) for i in range(1, last)])
    pad, part, gxs, gzs, token = call(
        lambda *refs: known_terms(nz, *refs),
        "known_terms",
        (pad, mh, came, came),
        [pad_shape, vmem(2, nz, columns, LANES), vmem(3, nz, padded, LANES), vmem(3, nz, columns, LANES), token_shape],
        [],
        80 * volume,
        8 * volume,
        4 * mib,
        aliases={0: 0},
    )
    pad, part, gxs, gzs = keep(pad, part, gxs, gzs)
    total, below, came = scan_step(1, total, below, token)

    level = 2
    while (1 << level) < n_gy:
        total, below, came = scan_step(level, total, below)
        level += 1

    (out,) = call(
        lambda *refs: finish(nz, last, *refs),
        "finish",
        (pad, v0, part, dwall, gxs, gzs, mh, vectors, matrix, masks, strip_a, strip_b, got_a, got_b, below, total, sums),
        [jax.ShapeDtypeStruct((3, nz, columns, rows_here), F32)],
        [
            vmem(nz, padded, LANES),
            vmem(3, nz, columns, LANES),
            vmem(24 * nz, LANES),
            half(2 * rows),
            half(4 * GROUP * columns),
            vmem(4 * GROUP * columns, LANES),
            vmem(GROUP, columns, LANES),
            pltpu.SemaphoreType.DMA((nz // GROUP,)),
        ],
        80 * volume,
        20 * volume,
        16 * mib,
    )
    return out


def solution(mesh):
    in_specs = (P(None, None, "gx", "gy"), P(), P())
    out_specs = P(None, None, "gx", "gy")
    return jax.shard_map(shards, mesh=mesh, in_specs=in_specs, out_specs=out_specs, check_vma=False)
```

time: 70.5 us -> 45.6 us (0.65)
  Pallas kernels: 37.5 us -> 24.6 us
  local copies, waits for them, and re-layouts: 9.16 us -> 1.07 us
  waiting for transfers between devices: 11.7 us -> 9.42 us
  starting transfers between devices: 11.5 us -> 10.1 us
    pallas_call x5, Pallas kernels: 37.5 us -> 24.6 us  [call(): pl.pallas_call(body, name=name, in_specs=[HBM if i in far else WHOLE for...]
    unnamed x14 -> x0, local copies, waits for them, and re-layouts: 8.08 us -> none
    ppermute x1, waiting for transfers between devices: 1.9 us -> 0.01 us  [shards(): xr = lax.ppermute(sent, 'gx', [(0, 1), (1, 0)])]
    ppermute x6, starting transfers between devices: 11.4 us -> 10.1 us  [the longest x4 6.31 us: scan_step(): came = lax.ppermute(total, 'gy', [(i, i ^ 1 << level) for i in range(n_gy)])]
  transfers between devices with their start and end apart: 7 -> 7, of which waited for: 4 -> 3; matrix products, arithmetic and copies ran while one was open for 0% -> 0% of each run, Pallas kernels for 19% -> 31%
where the time goes in v2:
time: 45.6 us; the launch traced here: 45.4 us
  Pallas kernels  24.6 us (54%)
  starting transfers between devices  10.1 us (22%)
  waiting for transfers between devices  9.42 us (21%)
  local copies, waits for them, and re-layouts  1.07 us (2%)
    pallas_call x5, Pallas kernels, call(): pl.pallas_call(body, name=name, in_specs=[HBM if i in far else WHOLE for...  24.6 us
    ppermute x4, starting transfers between devices, scan_step(): came = lax.ppermute(total, 'gy', [(i, i ^ 1 << level) for i in range(n_gy)])  6.31 us
    ppermute x4, waiting for transfers between devices, scan_step(): came = lax.ppermute(total, 'gy', [(i, i ^ 1 << level) for i in range(n_gy)])  3.87 us
    ppermute x1, starting transfers between devices, shards(): lax.ppermute(strip_b, 'gy', [(i, i + 1) if i % 2 else (i, i - 1) for i in...  3.21 us
    ppermute x1, waiting for transfers between devices, shards(): lax.ppermute(strip_b, 'gy', [(i, i + 1) if i % 2 else (i, i - 1) for i in...  3.03 us
    ppermute x1, waiting for transfers between devices, shards(): got_a = lax.ppermute(strip_a, 'gy', [(i, i ^ 1) for i in range(n_gy)])  2.53 us
    slice x1, local copies, waits for them, and re-layouts, shards(): velocity[:, :, :EDGE]  1.07 us
  transfers between devices with their start and end apart: 7, of which 3 were waited for; matrix products, arithmetic and copies ran while one was open for 0% of the time, Pallas kernels for 31%

profile of v2, /device:TPU:8, one launch (start us, length us, event | category | flops | bytes accessed | tf_op | source)
XLA Modules:
  0.0 45.4 jit_solution(6257746423395605630)
XLA Ops:
  0.0 1.1 %fusion = (f32[2,32,8,128]{3,2,1,0:T(8,128)S(1)}, f32[2,32,8,128]{3,2,1,0:T(8,128)S(1)}) fusion(f32[2,32,128,128]{3,2,1,0:T(8,128)} %refs_0_.1), kind=kLoop, calls=%fused_computation.8 | loop fusion | bytes 1048576 | tf_op jit(solution)/shard_map/slice | solution.py:531
  1.1 0.1 collective-permute-start
  1.2 3.0 %sum_rows.1 = (f32[2,32,144,128]{3,2,1,0:T(8,128)S(1)}, f32[128,128]{1,0:T(8,128)S(1)}, f32[144,128]{1,0:T(8,128)S(1)}, f32[144,128]{1,0:T(8,128)S(1)}, f32[8,12...) custom-call(f32[2,32,128,128]{3,2,1,0:T(8,128)} %refs_0_.1, ...), custom_call_target="tpu_custom_call" | custom-call | flops 2097152 | bytes 4194304 | tf_op jit(solution)/shard_map/sum_rows/pallas_call | solution.py:500
  4.2 0.0 collective-permute-done.refs_1_.refs_0_
  4.2 0.5 %sum_slopes.1.refs_16_ = f32[136,128]{1,0:T(8,128)S(1)} custom-call(f32[2,32,16,128]{3,2,1,0:T(8,128)S(1)} %collective-permute-done.refs_1_.refs_0_, f32[128,128]{1,0:T(8,128)S(1)} %get-tuple-element.30.refs_1_, f32[144,128]{1,0:T(8,128)S(1)} %get-tuple-element.25.refs_2_, f32[8,128]{1,0:T(8,128)S(1)} %get-tuple-element.26.refs_3_.refs_7_), custom_call_target="tpu_custom_call" | custom-call | flops 131072 | bytes 262144 | tf_op jit(solution)/shard_map/sum_slopes/pallas_call | solution.py:500
  4.8 1.6 %collective-permute-start.1 = (f32[136,128]{1,0:T(8,128)S(1)}, f32[136,128]{1,0:T(8,128)S(1)}, u32[]{:S(2)}, u32[]{:S(2)}) collective-permute-start(f32[136,128]{1,0:T(8,128)S(1)} %sum_slopes.1.refs_16_), channel_id=1, source_target_pairs={{0,1},{1,0},{2,3},{3,2},{4,5},{5,4},{6,7},{7,6},{8,9},{9,8},{10,11... | collective-permute-start | bytes 208904 | tf_op jit(solution)/shard_map/ppermute | solution.py:561
  6.3 5.8 %prepare.1 = (f32[2,32,144,128]{3,2,1,0:T(8,128)S(1)}, f32[32,144,128]{2,1,0:T(8,128)S(1)}, f32[2,32,128,128]{3,2,1,0:T(8,128)S(1)}, f32[288,128]{1,0:T(8,128)S(...) custom-call(f32[2,32,144,128]{3,2,1,0:T(8,128)S(1)} %get-tuple-element.24.refs_0_, ...), custom_call_target="tpu_custom_call", output_to_operand_aliasing={{0}: (0, {})} | custom-call | flops 31457280 | bytes 4194304 | tf_op jit(solution)/shard_map/prepare/pallas_call | solution.py:500
  12.2 0.0 collective-permute-done.1.refs_2_.refs_3_
  12.2 1.6 %collective-permute-start.4 = (f32[136,128]{1,0:T(8,128)S(1)}, f32[136,128]{1,0:T(8,128)S(1)}, u32[]{:S(2)}, u32[]{:S(2)}) collective-permute-start(f32[136,128]{1,0:T(8,128)S(1)} %add_add_fusion.1), channel_id=1, source_target_pairs={{0,2},{1,3},{2,0},{3,1},{4,6},{5,7},{6,4},{7,5},{8,10},{9,11},{10,... | collective-permute-start | bytes 208904 | tf_op jit(solution)/shard_map/ppermute | solution.py:561
  13.8 5.2 %known_terms.1 = (f32[2,32,144,128]{3,2,1,0:T(8,128)S(1)}, f32[2,32,128,128]{3,2,1,0:T(8,128)S(1)}, f32[3,32,144,128]{3,2,1,0:T(8,128)S(1)}, f32[3,32,128,128]{3,2,1,0:T(8,128)S(1)}, f32[136,128]{1,0:T(8,128)S(1)}) custom-call(f32[2,32,144,128]{3,2,1,0:T(8,128)S(1)} %get-tuple-element.28.refs_0_, ...), custom_call_target="tpu_custom_call", output_to_operand_aliasing={{0}: (0, {})} | custom-call | flops 41943040 | bytes 4194304 | tf_op jit(solution)/shard_map/known_terms/pallas_call | solution.py:500
  19.0 0.0 collective-permute-done.4
  19.0 0.5 %collective-permute-start.5 = (f32[136,128]{1,0:T(8,128)S(1)}, f32[136,128]{1,0:T(8,128)S(1)}, u32[]{:S(2)}, u32[]{:S(2)}) collective-permute-start(f32[136,128]{1,0:T(8,128)S(1)} %add_add_fusion), channel_id=1, source_target_pairs={{0,4},{1,5},{2,6},{3,7},{4,0},{5,1},{6,2},{7,3},{8,12},{9,13},{10,... | collective-permute-start | bytes 208904 | tf_op jit(solution)/shard_map/ppermute | solution.py:561
  19.5 3.9 %collective-permute-done.5 = f32[136,128]{1,0:T(8,128)S(1)} collective-permute-done((f32[136,128]{1,0:T(8,128)S(1)}, f32[136,128]{1,0:T(8,128)S(1)}, u32[]{:S(2)}, u32[]{:S(2)}) %collective-permute-start.5) | collective-permute-done | bytes 69664 | tf_op jit(solution)/shard_map/ppermute | solution.py:561
  23.4 2.7 %collective-permute-start.6 = (f32[136,128]{1,0:T(8,128)S(1)}, f32[136,128]{1,0:T(8,128)S(1)}, u32[]{:S(2)}, u32[]{:S(2)}) collective-permute-start(f32[136,128]{1,0:T(8,128)S(1)} %add.33), channel_id=1, source_target_pairs={{0,8},{1,9},{2,10},{3,11},{4,12},{5,13},{6,14},{7,15},{8,0},{9,1},... | collective-permute-start | bytes 208904 | tf_op jit(solution)/shard_map/ppermute | solution.py:561
  26.1 0.5 %collective-permute-start.2 = (f32[288,128]{1,0:T(8,128)S(1)}, f32[288,128]{1,0:T(8,128)S(1)}, u32[]{:S(2)}, u32[]{:S(2)}) collective-permute-start(f32[288,128]{1,0:T(8,128)S(1)} %get-tuple-element.38.refs_10_), channel_id=1, source_target_pairs={{0,1},{1,0},{2,3},{3,2},{4,5},{5,4},{6,7},{7,6},{8,9},{9,8},{10,11... | collective-permute-start | bytes 442376 | tf_op jit(solution)/shard_map/ppermute | solution.py:582
  26.6 3.2 %collective-permute-start.3 = (f32[288,128]{1,0:T(8,128)S(1)}, f32[288,128]{1,0:T(8,128)S(1)}, u32[]{:S(2)}, u32[]{:S(2)}) collective-permute-start(f32[288,128]{1,0:T(8,128)S(1)} %get-tuple-element.39.refs_11_), channel_id=1, source_target_pairs={{1,2},{2,1},{3,4},{4,3},{5,6},{6,5},{7,8},{8,7},{9,10},{10,9},{11,... | collective-permute-start | bytes 442376 | tf_op jit(solution)/shard_map/ppermute | solution.py:583
  29.8 0.0 collective-permute-done.6
  29.9 2.5 %collective-permute-done.2.refs_12_ = f32[288,128]{1,0:T(8,128)S(1)} collective-permute-done((f32[288,128]{1,0:T(8,128)S(1)}, f32[288,128]{1,0:T(8,128)S(1)}, u32[]{:S(2)}, u32[]{:S(2)}) %collective-permute-start.2) | collective-permute-done | bytes 147488 | tf_op jit(solution)/shard_map/ppermute | solution.py:582
  32.4 3.0 %collective-permute-done.3.refs_13_ = f32[288,128]{1,0:T(8,128)S(1)} collective-permute-done((f32[288,128]{1,0:T(8,128)S(1)}, f32[288,128]{1,0:T(8,128)S(1)}, u32[]{:S(2)}, u32[]{:S(2)}) %collective-permute-start.3) | collective-permute-done | bytes 147488 | tf_op jit(solution)/shard_map/ppermute | solution.py:583
  35.4 10.0 %finish.1 = f32[3,32,128,128]{3,2,1,0:T(8,128)} custom-call(f32[2,32,144,128]{3,2,1,0:T(8,128)S(1)} %get-tuple-element.31.refs_0_, f32[32,144,128]{2,1,0:T(8,128)S(1)} %get-tuple-element.32.refs_1_, f32[2,32,128,128]{3,2,1,0:T(8,128)S(1)} %get-tuple-element.33.refs_2_, f32[2,32,128,128]{3,2,1,0:T(8,128)S(1)} %get-tuple-element.34.refs_3_, ...), custom_call_target="tpu_custom_call" | custom-call | flops 41943040 | bytes 10485760 | tf_op jit(solution)/shard_map/finish/pallas_call | solution.py:500
  (6 shorter events, 0.1 us)
Async XLA Ops:
  1.1 3.1 %collective-permute-start = (f32[2,32,16,128]{3,2,1,0:T(8,128)S(1)}, f32[2,32,16,128]{3,2,1,0:T(8,128)S(1)}, u32[]{:S(2)}, u32[]{:S(2)}) collective-permute-start(f32[2,32,16,128]{3,2,1,0:T(8,128)S(1)} %pad_maximum_fusion), channel_id=1, source_target_pairs={{0,16},{16,0},{1,17},{17,1},{2,18},{18,2},{3,19},{19,3},{4,20},{20... | collective-permute-start | bytes 1572872 | tf_op jit(solution)/shard_map/ppermute | solution.py:532
  4.8 7.4 %collective-permute-start.1 = (f32[136,128]{1,0:T(8,128)S(1)}, f32[136,128]{1,0:T(8,128)S(1)}, u32[]{:S(2)}, u32[]{:S(2)}) collective-permute-start(f32[136,128]{1,0:T(8,128)S(1)} %sum_slopes.1.refs_16_), channel_id=1, source_target_pairs={{0,1},{1,0},{2,3},{3,2},{4,5},{5,4},{6,7},{7,6},{8,9},{9,8},{10,11... | collective-permute-start | bytes 208904 | tf_op jit(solution)/shard_map/ppermute | solution.py:561
  12.2 6.8 %collective-permute-start.4 = (f32[136,128]{1,0:T(8,128)S(1)}, f32[136,128]{1,0:T(8,128)S(1)}, u32[]{:S(2)}, u32[]{:S(2)}) collective-permute-start(f32[136,128]{1,0:T(8,128)S(1)} %add_add_fusion.1), channel_id=1, source_target_pairs={{0,2},{1,3},{2,0},{3,1},{4,6},{5,7},{6,4},{7,5},{8,10},{9,11},{10,... | collective-permute-start | bytes 208904 | tf_op jit(solution)/shard_map/ppermute | solution.py:561
  19.0 4.4 %collective-permute-start.5 = (f32[136,128]{1,0:T(8,128)S(1)}, f32[136,128]{1,0:T(8,128)S(1)}, u32[]{:S(2)}, u32[]{:S(2)}) collective-permute-start(f32[136,128]{1,0:T(8,128)S(1)} %add_add_fusion), channel_id=1, source_target_pairs={{0,4},{1,5},{2,6},{3,7},{4,0},{5,1},{6,2},{7,3},{8,12},{9,13},{10,... | collective-permute-start | bytes 208904 | tf_op jit(solution)/shard_map/ppermute | solution.py:561
  23.4 6.4 %collective-permute-start.6 = (f32[136,128]{1,0:T(8,128)S(1)}, f32[136,128]{1,0:T(8,128)S(1)}, u32[]{:S(2)}, u32[]{:S(2)}) collective-permute-start(f32[136,128]{1,0:T(8,128)S(1)} %add.33), channel_id=1, source_target_pairs={{0,8},{1,9},{2,10},{3,11},{4,12},{5,13},{6,14},{7,15},{8,0},{9,1},... | collective-permute-start | bytes 208904 | tf_op jit(solution)/shard_map/ppermute | solution.py:561
  26.1 6.3 %collective-permute-start.2 = (f32[288,128]{1,0:T(8,128)S(1)}, f32[288,128]{1,0:T(8,128)S(1)}, u32[]{:S(2)}, u32[]{:S(2)}) collective-permute-start(f32[288,128]{1,0:T(8,128)S(1)} %get-tuple-element.38.refs_10_), channel_id=1, source_target_pairs={{0,1},{1,0},{2,3},{3,2},{4,5},{5,4},{6,7},{7,6},{8,9},{9,8},{10,11... | collective-permute-start | bytes 442376 | tf_op jit(solution)/shard_map/ppermute | solution.py:582
  26.6 8.8 %collective-permute-start.3 = (f32[288,128]{1,0:T(8,128)S(1)}, f32[288,128]{1,0:T(8,128)S(1)}, u32[]{:S(2)}, u32[]{:S(2)}) collective-permute-start(f32[288,128]{1,0:T(8,128)S(1)} %get-tuple-element.39.refs_11_), channel_id=1, source_target_pairs={{1,2},{2,1},{3,4},{4,3},{5,6},{6,5},{7,8},{8,7},{9,10},{10,9},{11,... | collective-permute-start | bytes 442376 | tf_op jit(solution)/shard_map/ppermute | solution.py:583

commit v3 on v2

--- a/solution.py
+++ b/solution.py
@@ -75,7 +75,7 @@
     gx = lax.axis_index("gx")
     gy = lax.axis_index("gy")
     columns = uw.shape[0]
-    chunks = 8
+    chunks = 4
     per = nz // chunks
 
     def chunk(c):
@@ -162,10 +162,9 @@
 
 
 def prepare(
-    nz, pad_in, xr, ms, vectors, matrix, pad, v0, dwall, strip_a, strip_b, token,
+    nz, first, count, pad, ms, vectors, matrix, v0, dwall, strip_a, strip_b, token,
     weights_s, weights_u, weights_w, halves_s, halves_u, halves_w, edges, turned,
 ):
-    del pad_in
     gy = lax.axis_index("gy")
     columns = dwall.shape[2]
     rows = columns + EDGE
@@ -183,8 +182,6 @@
     weights_w[:, LANES:] = edge_columns(6)
     odd = lax.rem(gy, 2) == 1
     token[...] = jnp.zeros(token.shape, F32)
-    pad[:, :, pl.ds(0, EDGE), :] = xr[:, :, pl.ds(EDGE, EDGE), :]
-    pad[:, :, pl.ds(EDGE + columns, EDGE), :] = xr[:, :, pl.ds(0, EDGE), :]
 
     def gather(g):
         blocks = []
@@ -225,30 +222,50 @@
             packed = made_u[at, LANES:] + made_w[at, LANES:] + edges[p, pl.ds(3, columns), :]
             turned[p] = packed.T[:24]
             for f in range(3):
-                last = turned[p, 6 * f : 6 * f + 3, :]
-                first = turned[p, 6 * f + 3 : 6 * f + 6, :]
-                strip_a[pl.ds(3 * f * nz + z, 3, stride=nz), :] = jnp.where(odd, first, last)
-                strip_b[pl.ds(3 * f * nz + z, 3, stride=nz), :] = jnp.where(odd, last, first)
+                high = turned[p, 6 * f : 6 * f + 3, :]
+                low = turned[p, 6 * f + 3 : 6 * f + 6, :]
+                strip_a[pl.ds(3 * f * nz + z, 3, stride=nz), :] = jnp.where(odd, low, high)
+                strip_b[pl.ds(3 * f * nz + z, 3, stride=nz), :] = jnp.where(odd, high, low)
 
     def step(g, _):
         settle(g)
         gather(g + 1)
         return 0
 
-    groups = nz // GROUP
-    gather(0)
-    lax.fori_loop(0, groups - 1, step, 0)
-    settle(groups - 1)
-
-
-def known_terms(nz, pad, mh, wait_a, wait_b, pad_out, part, gx_out, gz_out, token):
-    del pad_out, wait_a, wait_b
-    columns = part.shape[2]
-    token[...] = jnp.zeros(token.shape, F32)
+    gather(first)
+    lax.fori_loop(first, first + count - 1, step, 0)
+    settle(first + count - 1)
+
+
+def prepare_first(nz, first, count, pad_in, xr, ms, vectors, matrix, pad, *rest):
+    del pad_in
+    columns = pad.shape[2] - 2 * EDGE
+    pad[:, :, pl.ds(0, EDGE), :] = xr[:, :, pl.ds(EDGE, EDGE), :]
+    pad[:, :, pl.ds(EDGE + columns, EDGE), :] = xr[:, :, pl.ds(0, EDGE), :]
+    prepare(nz, first, count, pad, ms, vectors, matrix, *rest)
+
+
+def prepare_last(nz, first, count, pad, v0, dwall, strip_a, strip_b, ms, vectors, matrix, wait, *rest):
+    del v0, dwall, strip_a, strip_b, wait
+    prepare(nz, first, count, pad, ms, vectors, matrix, *rest)
+
+
+def known_first(nz, count, pad, mh, wait, part, gx_out, gz_out, token):
+    del wait
     for z in range(nz):
         u = pad[0, z, pl.ds(0, 8), :]
         for distance, weight in CENTRAL:
             gx_out[distance - 1, z, pl.ds(0, 8), :] = weight * (u + pad[0, z, pl.ds(distance, 8), :])
+    known_terms(nz, 0, count, pad, mh, part, gx_out, gz_out, token)
+
+
+def known_last(nz, first, pad, part_in, gx_in, gz_in, mh, wait_a, wait_b, wait_c, part, gx_out, gz_out, token):
+    del part_in, gx_in, gz_in, wait_a, wait_b, wait_c
+    known_terms(nz, first, part.shape[2] // 8 - first, pad, mh, part, gx_out, gz_out, token)
+
+
+def known_terms(nz, first, count, pad, mh, part, gx_out, gz_out, token):
+    token[...] = jnp.zeros(token.shape, F32)
 
     def block(k, _):
         r = pl.multiple_of(8 * k + EDGE, 8)
@@ -290,7 +307,7 @@
                 part[c, z, at, :] = across[c] * metric + along[c]
         return 0
 
-    lax.fori_loop(0, columns // 8, block, 0)
+    lax.fori_loop(first, first + count, block, 0)
 
 
 def finish(
@@ -482,16 +499,22 @@
         planes = pl.ds(g * GROUP, GROUP)
         return pltpu.make_async_copy(buf.at[:, planes], out.at[:, planes], sems.at[g])
 
-    def step(g, _):
+    def step(g, _=None, ahead=3):
         complete(g)
-        make_slopes()
-        make_turned(wrapped(g + 1, groups))
-        make_halves(wrapped(g + 2, groups))
-        make_v(wrapped(g + 3, groups))
         send(g).start()
+        if ahead > 0:
+            make_slopes()
+            make_turned(g + 1)
+        if ahead > 1:
+            make_halves(g + 2)
+        if ahead > 2:
+            make_v(g + 3)
         return 0
 
-    lax.fori_loop(0, groups, step, 0)
+    for g in range(groups - 4):
+        step(g)
+    for g, ahead in ((groups - 4, 2), (groups - 3, 2), (groups - 2, 1), (groups - 1, 0)):
+        step(g, ahead=ahead)
     for g in range(groups):
         send(g).wait()
 
@@ -539,7 +562,7 @@
         "sum_rows",
         (near, metric, wall),
         [pad_shape, vmem(columns, LANES), vmem(padded, LANES), vmem(padded, LANES), vmem(8, LANES), pltpu.VMEM((2 * LANES, LANES), BF16), vmem(8, LANES), pltpu.VMEM((8 * nz, 2 * LANES), BF16)],
-        [vmem(2, columns), vmem(n_gy, rows_here), pltpu.SemaphoreType.DMA((10,))],
+        [vmem(2, columns), vmem(n_gy, rows_here), pltpu.SemaphoreType.DMA((6,))],
         4 * volume,
         8 * volume,
         2 * mib,
@@ -564,38 +587,74 @@
         return (total if token is None else total + token), below, came
 
     half = lambda count: pltpu.VMEM((count, 2 * LANES), BF16)
+    groups = nz // GROUP
+    blocks = columns // 8
+    first_groups, first_blocks = groups // 2, blocks // 2
+    half = lambda count: pltpu.VMEM((count, 2 * LANES), BF16)
+    prepared = [vmem(nz, padded, LANES), vmem(2, nz, columns, LANES), vmem(9 * nz, LANES), vmem(9 * nz, LANES), token_shape]
+    prepare_scratch = [half(2 * LANES)] * 3 + [
+        half(GROUP * rows),
+        half(GROUP * columns),
+        half(GROUP * columns),
+        vmem(GROUP, rows, LANES),
+        vmem(GROUP, 24, LANES),
+    ]
     pad, v0, dwall, strip_a, strip_b, token = call(
-        lambda *refs: prepare(nz, *refs),
-        "prepare",
+        lambda *refs: prepare_first(nz, 0, first_groups, *refs),
+        "prepare_first",
         (pad, xr, ms, vectors, matrix),
-        [pad_shape, vmem(nz, padded, LANES), vmem(2, nz, columns, LANES), vmem(9 * nz, LANES), vmem(9 * nz, LANES), token_shape],
-        [half(2 * LANES)] * 3
-        + [half(GROUP * rows), half(GROUP * columns), half(GROUP * columns), vmem(GROUP, rows, LANES), vmem(GROUP, 24, LANES)],
-        60 * volume,
-        8 * volume,
+        [pad_shape] + prepared,
+        prepare_scratch,
+        30 * volume,
+        4 * volume,
         6 * mib,
         aliases={0: 0},
     )
-    pad, v0, dwall = keep(pad, v0, dwall)
+    pad, v0, dwall, strip_a, strip_b = keep(pad, v0, dwall, strip_a, strip_b)
     total, below, came = scan_step(0, sums, jnp.zeros_like(sums), token)
+    v0, dwall, strip_a, strip_b, token = call(
+        lambda *refs: prepare_last(nz, first_groups, groups - first_groups, *refs),
+        "prepare_last",
+        (pad, v0, dwall, strip_a, strip_b, ms, vectors, matrix, came),
+        prepared,
+        prepare_scratch,
+        30 * volume,
+        4 * volume,
+        6 * mib,
+        aliases={1: 0, 2: 1, 3: 2, 4: 3},
+    )
+    v0, dwall = keep(v0, dwall)
+    total, below, came = scan_step(1, total, below, token)
 
     got_a = lax.ppermute(strip_a, "gy", [(i, i ^ 1) for i in range(n_gy)])
     got_b = lax.ppermute(strip_b, "gy", [(i, i + 1) if i % 2 else (i, i - 1) for i in range(1, last)])
-    pad, part, gxs, gzs, token = call(
-        lambda *refs: known_terms(nz, *refs),
-        "known_terms",
-        (pad, mh, came, came),
-        [pad_shape, vmem(2, nz, columns, LANES), vmem(3, nz, padded, LANES), vmem(3, nz, columns, LANES), token_shape],
+    known = [vmem(2, nz, columns, LANES), vmem(3, nz, padded, LANES), vmem(3, nz, columns, LANES), token_shape]
+    part, gxs, gzs, token = call(
+        lambda *refs: known_first(nz, first_blocks, *refs),
+        "known_first",
+        (pad, mh, came),
+        known,
         [],
-        80 * volume,
-        8 * volume,
+        40 * volume,
+        4 * volume,
         4 * mib,
-        aliases={0: 0},
-    )
-    pad, part, gxs, gzs = keep(pad, part, gxs, gzs)
-    total, below, came = scan_step(1, total, below, token)
-
-    level = 2
+    )
+    part, gxs, gzs = keep(part, gxs, gzs)
+    total, below, came = scan_step(2, total, below, token)
+    part, gxs, gzs, token = call(
+        lambda *refs: known_last(nz, first_blocks, *refs),
+        "known_last",
+        (pad, part, gxs, gzs, mh, came, got_a, got_b),
+        known,
+        [],
+        40 * volume,
+        4 * volume,
+        4 * mib,
+        aliases={1: 0, 2: 1, 3: 2},
+    )
+    part, gxs, gzs = keep(part, gxs, gzs)
+
+    level = 3
     while (1 << level) < n_gy:
         total, below, came = scan_step(level, total, below)
         level += 1

time: 45.6 us -> 39.3 us (0.86)
  the two profiles are of different devices: /device:TPU:8 before, /device:TPU:16 now
where the time goes in v3:
time: 39.3 us; the launch traced here: 39.1 us
  Pallas kernels  23.7 us (60%)
  starting transfers between devices  8.41 us (21%)
  waiting for transfers between devices  5.68 us (14%)
  local copies, waits for them, and re-layouts  1.07 us (3%)
    pallas_call x7, Pallas kernels, call(): pl.pallas_call(body, name=name, in_specs=[HBM if i in far else WHOLE for...  23.7 us
    ppermute x1, waiting for transfers between devices, shards(): lax.ppermute(strip_b, 'gy', [(i, i + 1) if i % 2 else (i, i - 1) for i in...  5.54 us
    ppermute x4, starting transfers between devices, scan_step(): came = lax.ppermute(total, 'gy', [(i, i ^ 1 << level) for i in range(n_gy)])  4.85 us
    ppermute x1, starting transfers between devices, shards(): lax.ppermute(strip_b, 'gy', [(i, i + 1) if i % 2 else (i, i - 1) for i in...  1.98 us
    ppermute x1, starting transfers between devices, shards(): got_a = lax.ppermute(strip_a, 'gy', [(i, i ^ 1) for i in range(n_gy)])  1.5 us
    slice x1, local copies, waits for them, and re-layouts, shards(): velocity[:, :, :EDGE]  1.07 us
  transfers between devices with their start and end apart: 7, of which 2 were waited for; matrix products, arithmetic and copies ran while one was open for 0% of the time, Pallas kernels for 37%

profile of v3, /device:TPU:16, one launch (start us, length us, event | category | flops | bytes accessed | tf_op | source)
XLA Modules:
  0.0 39.1 jit_solution(1372675323253586118)
XLA Ops:
  0.0 1.1 %fusion = (f32[2,32,8,128]{3,2,1,0:T(8,128)S(1)}, f32[2,32,8,128]{3,2,1,0:T(8,128)S(1)}) fusion(f32[2,32,128,128]{3,2,1,0:T(8,128)} %refs_0_.1), kind=kLoop, calls=%fused_computation.9 | loop fusion | bytes 1048576 | tf_op jit(solution)/shard_map/slice | solution.py:554
  1.1 0.1 collective-permute-start
  1.2 2.7 %sum_rows.1 = (f32[2,32,144,128]{3,2,1,0:T(8,128)S(1)}, f32[128,128]{1,0:T(8,128)S(1)}, f32[144,128]{1,0:T(8,128)S(1)}, f32[144,128]{1,0:T(8,128)S(1)}, f32[8,12...) custom-call(f32[2,32,128,128]{3,2,1,0:T(8,128)} %refs_0_.1, ...), custom_call_target="tpu_custom_call" | custom-call | flops 2097152 | bytes 4194304 | tf_op jit(solution)/shard_map/sum_rows/pallas_call | solution.py:523
  3.9 0.0 collective-permute-done.refs_1_.refs_0_
  3.9 0.5 %sum_slopes.1.refs_16_ = f32[136,128]{1,0:T(8,128)S(1)} custom-call(f32[2,32,16,128]{3,2,1,0:T(8,128)S(1)} %collective-permute-done.refs_1_.refs_0_, f32[128,128]{1,0:T(8,128)S(1)} %get-tuple-element.40.refs_1_, f32[144,128]{1,0:T(8,128)S(1)} %get-tuple-element.32.refs_2_.refs_5_, f32[8,128]{1,0:T(8,128)S(1)} %get-tuple-element.33.refs_3_.refs_6_.refs_7_), custom_call_target="tpu_custom_call" | custom-call | flops 131072 | bytes 262144 | tf_op jit(solution)/shard_map/sum_slopes/pallas_call | solution.py:523
  4.5 1.6 %collective-permute-start.1 = (f32[136,128]{1,0:T(8,128)S(1)}, f32[136,128]{1,0:T(8,128)S(1)}, u32[]{:S(2)}, u32[]{:S(2)}) collective-permute-start(f32[136,128]{1,0:T(8,128)S(1)} %sum_slopes.1.refs_16_), channel_id=1, source_target_pairs={{0,1},{1,0},{2,3},{3,2},{4,5},{5,4},{6,7},{7,6},{8,9},{9,8},{10,11... | collective-permute-start | bytes 208904 | tf_op jit(solution)/shard_map/ppermute | solution.py:584
  6.0 3.0 %prepare_first.1 = (f32[2,32,144,128]{3,2,1,0:T(8,128)S(1)}, f32[32,144,128]{2,1,0:T(8,128)S(1)}, f32[2,32,128,128]{3,2,1,0:T(8,128)S(1)}, f32[288,128]{1,0:T(8,...) custom-call(f32[2,32,144,128]{3,2,1,0:T(8,128)S(1)} %get-tuple-element.31.refs_0_, ...), custom_call_target="tpu_custom_call", output_to_operand_aliasing={{0}: (0, {})} | custom-call | flops 15728640 | bytes 2097152 | tf_op jit(solution)/shard_map/prepare_first/pallas_call | solution.py:523
  9.0 0.1 collective-permute-done.1.refs_8_
  9.1 1.6 %collective-permute-start.2 = (f32[136,128]{1,0:T(8,128)S(1)}, f32[136,128]{1,0:T(8,128)S(1)}, u32[]{:S(2)}, u32[]{:S(2)}) collective-permute-start(f32[136,128]{1,0:T(8,128)S(1)} %add_add_fusion.2), channel_id=1, source_target_pairs={{0,2},{1,3},{2,0},{3,1},{4,6},{5,7},{6,4},{7,5},{8,10},{9,11},{10,... | collective-permute-start | bytes 208904 | tf_op jit(solution)/shard_map/ppermute | solution.py:584
  10.7 2.9 %prepare_last.1 = (f32[32,144,128]{2,1,0:T(8,128)S(1)}, f32[2,32,128,128]{3,2,1,0:T(8,128)S(1)}, f32[288,128]{1,0:T(8,128)S(1)}, f32[288,128]{1,0:T(8,128)S(1)}, f32[136,128]{1,0:T(8,128)S(1)}) custom-call(f32[2,32,144,128]{3,2,1,0:T(8,128)S(1)} %get-tuple-element.35.refs_0_, ...), custom_call_target="tpu_custom_call", output_to_operand_aliasing={{0}: (1, {}), {1}: (2, {}), {2}: (3, {}), {3}: (4, {})} | custom-call | flops 15728640 | bytes 2097152 | tf_op jit(solution)/shard_map/prepare_last/pallas_call | solution.py:523
  13.6 0.0 collective-permute-done.2.refs_2_
  13.7 1.6 %collective-permute-start.3 = (f32[136,128]{1,0:T(8,128)S(1)}, f32[136,128]{1,0:T(8,128)S(1)}, u32[]{:S(2)}, u32[]{:S(2)}) collective-permute-start(f32[136,128]{1,0:T(8,128)S(1)} %add_add_fusion.1), channel_id=1, source_target_pairs={{0,4},{1,5},{2,6},{3,7},{4,0},{5,1},{6,2},{7,3},{8,12},{9,13},{10,... | collective-permute-start | bytes 208904 | tf_op jit(solution)/shard_map/ppermute | solution.py:584
  15.3 1.5 %collective-permute-start.4 = (f32[288,128]{1,0:T(8,128)S(1)}, f32[288,128]{1,0:T(8,128)S(1)}, u32[]{:S(2)}, u32[]{:S(2)}) collective-permute-start(f32[288,128]{1,0:T(8,128)S(1)} %get-tuple-element.48.refs_10_), channel_id=1, source_target_pairs={{0,1},{1,0},{2,3},{3,2},{4,5},{5,4},{6,7},{7,6},{8,9},{9,8},{10,11... | collective-permute-start | bytes 442376 | tf_op jit(solution)/shard_map/ppermute | solution.py:629
  16.8 2.0 %collective-permute-start.5 = (f32[288,128]{1,0:T(8,128)S(1)}, f32[288,128]{1,0:T(8,128)S(1)}, u32[]{:S(2)}, u32[]{:S(2)}) collective-permute-start(f32[288,128]{1,0:T(8,128)S(1)} %get-tuple-element.49.refs_11_), channel_id=1, source_target_pairs={{1,2},{2,1},{3,4},{4,3},{5,6},{6,5},{7,8},{8,7},{9,10},{10,9},{11,... | collective-permute-start | bytes 442376 | tf_op jit(solution)/shard_map/ppermute | solution.py:630
  18.8 2.6 %known_first.1 = (f32[2,32,128,128]{3,2,1,0:T(8,128)S(1)}, f32[3,32,144,128]{3,2,1,0:T(8,128)S(1)}, f32[3,32,128,128]{3,2,1,0:T(8,128)S(1)}, f32[136,128]{1,0:T(8,128)S(1)}) custom-call(f32[2,32,144,128]{3,2,1,0:T(8,128)S(1)} %get-tuple-element.35.refs_0_, f32[144,128]{1,0:T(8,128)S(1)} %get-tuple-element.42.refs_1_.refs_4_.refs_6_, ...), custom_call_target="tpu_custom_call" | custom-call | flops 20971520 | bytes 2097152 | tf_op jit(solution)/shard_map/known_first/pallas_call | solution.py:523
  21.4 0.0 collective-permute-done.3.refs_5_
  21.5 0.1 collective-permute-start.6
  21.6 0.0 collective-permute-done.4.refs_6_.refs_12_
  21.6 5.5 %collective-permute-done.5.refs_7_.refs_13_ = f32[288,128]{1,0:T(8,128)S(1)} collective-permute-done((f32[288,128]{1,0:T(8,128)S(1)}, f32[288,128]{1,0:T(8,128)S(1)}, u32[]{:S(2)}, u32[]{:S(2)}) %collective-permute-start.5) | collective-permute-done | bytes 147488 | tf_op jit(solution)/shard_map/ppermute | solution.py:630
  27.1 3.2 %known_last.1 = (f32[2,32,128,128]{3,2,1,0:T(8,128)S(1)}, f32[3,32,144,128]{3,2,1,0:T(8,128)S(1)}, f32[3,32,128,128]{3,2,1,0:T(8,128)S(1)}, f32[136,128]{1,0:T(8,128)}) custom-call(f32[2,32,144,128]{3,2,1,0:T(8,128)S(1)} %get-tuple-element.35.refs_0_, ...), custom_call_target="tpu_custom_call", output_to_operand_aliasing={{0}: (1, {}), {1}: (2, {}), {2}: (3, {})} | custom-call | flops 20971520 | bytes 2097152 | tf_op jit(solution)/shard_map/known_last/pallas_call | solution.py:523
  30.3 0.0 collective-permute-done.6
  30.4 8.7 %finish.1 = f32[3,32,128,128]{3,2,1,0:T(8,128)} custom-call(f32[2,32,144,128]{3,2,1,0:T(8,128)S(1)} %get-tuple-element.35.refs_0_, f32[32,144,128]{2,1,0:T(8,128)S(1)} %get-tuple-element.41.refs_1_, f32[2,32,128,128]{3,2,1,0:T(8,128)S(1)} %get-tuple-element.50.refs_2_, f32[2,32,128,128]{3,2,1,0:T(8,128)S(1)} %get-tuple-element.51.refs_3_, ...), custom_call_target="tpu_custom_call" | custom-call | flops 41943040 | bytes 10485760 | tf_op jit(solution)/shard_map/finish/pallas_call | solution.py:523
  (6 shorter events, 0.1 us)
Async XLA Ops:
  1.1 2.8 %collective-permute-start = (f32[2,32,16,128]{3,2,1,0:T(8,128)S(1)}, f32[2,32,16,128]{3,2,1,0:T(8,128)S(1)}, u32[]{:S(2)}, u32[]{:S(2)}) collective-permute-start(f32[2,32,16,128]{3,2,1,0:T(8,128)S(1)} %pad_maximum_fusion), channel_id=1, source_target_pairs={{0,16},{16,0},{1,17},{17,1},{2,18},{18,2},{3,19},{19,3},{4,20},{20... | collective-permute-start | bytes 1572872 | tf_op jit(solution)/shard_map/ppermute | solution.py:555
  4.5 4.6 %collective-permute-start.1 = (f32[136,128]{1,0:T(8,128)S(1)}, f32[136,128]{1,0:T(8,128)S(1)}, u32[]{:S(2)}, u32[]{:S(2)}) collective-permute-start(f32[136,128]{1,0:T(8,128)S(1)} %sum_slopes.1.refs_16_), channel_id=1, source_target_pairs={{0,1},{1,0},{2,3},{3,2},{4,5},{5,4},{6,7},{7,6},{8,9},{9,8},{10,11... | collective-permute-start | bytes 208904 | tf_op jit(solution)/shard_map/ppermute | solution.py:584
  9.1 4.5 %collective-permute-start.2 = (f32[136,128]{1,0:T(8,128)S(1)}, f32[136,128]{1,0:T(8,128)S(1)}, u32[]{:S(2)}, u32[]{:S(2)}) collective-permute-start(f32[136,128]{1,0:T(8,128)S(1)} %add_add_fusion.2), channel_id=1, source_target_pairs={{0,2},{1,3},{2,0},{3,1},{4,6},{5,7},{6,4},{7,5},{8,10},{9,11},{10,... | collective-permute-start | bytes 208904 | tf_op jit(solution)/shard_map/ppermute | solution.py:584
  13.7 7.8 %collective-permute-start.3 = (f32[136,128]{1,0:T(8,128)S(1)}, f32[136,128]{1,0:T(8,128)S(1)}, u32[]{:S(2)}, u32[]{:S(2)}) collective-permute-start(f32[136,128]{1,0:T(8,128)S(1)} %add_add_fusion.1), channel_id=1, source_target_pairs={{0,4},{1,5},{2,6},{3,7},{4,0},{5,1},{6,2},{7,3},{8,12},{9,13},{10,... | collective-permute-start | bytes 208904 | tf_op jit(solution)/shard_map/ppermute | solution.py:584
  15.3 6.3 %collective-permute-start.4 = (f32[288,128]{1,0:T(8,128)S(1)}, f32[288,128]{1,0:T(8,128)S(1)}, u32[]{:S(2)}, u32[]{:S(2)}) collective-permute-start(f32[288,128]{1,0:T(8,128)S(1)} %get-tuple-element.48.refs_10_), channel_id=1, source_target_pairs={{0,1},{1,0},{2,3},{3,2},{4,5},{5,4},{6,7},{7,6},{8,9},{9,8},{10,11... | collective-permute-start | bytes 442376 | tf_op jit(solution)/shard_map/ppermute | solution.py:629
  16.8 10.3 %collective-permute-start.5 = (f32[288,128]{1,0:T(8,128)S(1)}, f32[288,128]{1,0:T(8,128)S(1)}, u32[]{:S(2)}, u32[]{:S(2)}) collective-permute-start(f32[288,128]{1,0:T(8,128)S(1)} %get-tuple-element.49.refs_11_), channel_id=1, source_target_pairs={{1,2},{2,1},{3,4},{4,3},{5,6},{6,5},{7,8},{8,7},{9,10},{10,9},{11,... | collective-permute-start | bytes 442376 | tf_op jit(solution)/shard_map/ppermute | solution.py:630
  21.5 8.9 %collective-permute-start.6 = (f32[136,128]{1,0:T(8,128)S(1)}, f32[136,128]{1,0:T(8,128)S(1)}, u32[]{:S(2)}, u32[]{:S(2)}) collective-permute-start(f32[136,128]{1,0:T(8,128)S(1)} %add_add_fusion), channel_id=1, source_target_pairs={{0,8},{1,9},{2,10},{3,11},{4,12},{5,13},{6,14},{7,15},{8,0},{9,1},... | collective-permute-start | bytes 208904 | tf_op jit(solution)/shard_map/ppermute | solution.py:584

commit v4 on v3

--- a/solution.py
+++ b/solution.py
@@ -644,7 +644,7 @@
     part, gxs, gzs, token = call(
         lambda *refs: known_last(nz, first_blocks, *refs),
         "known_last",
-        (pad, part, gxs, gzs, mh, came, got_a, got_b),
+        (pad, part, gxs, gzs, mh, came, got_a, came),
         known,
         [],
         40 * volume,

time: 39.3 us -> 38.9 us (0.990)
  the two profiles are of different devices: /device:TPU:16 before, /device:TPU:8 now
where the time goes in v4:
time: 38.9 us; the launch traced here: 38.6 us
  Pallas kernels  23.7 us (61%)
  starting transfers between devices  12.1 us (31%)
  waiting for transfers between devices  1.46 us (4%)
  local copies, waits for them, and re-layouts  1.07 us (3%)
    pallas_call x7, Pallas kernels, call(): pl.pallas_call(body, name=name, in_specs=[HBM if i in far else WHOLE for...  23.7 us
    ppermute x4, starting transfers between devices, scan_step(): came = lax.ppermute(total, 'gy', [(i, i ^ 1 << level) for i in range(n_gy)])  6.32 us
    ppermute x1, starting transfers between devices, shards(): lax.ppermute(strip_b, 'gy', [(i, i + 1) if i % 2 else (i, i - 1) for i in...  4.22 us
    ppermute x1, starting transfers between devices, shards(): got_a = lax.ppermute(strip_a, 'gy', [(i, i ^ 1) for i in range(n_gy)])  1.48 us
    ppermute x1, waiting for transfers between devices, shards(): lax.ppermute(strip_b, 'gy', [(i, i + 1) if i % 2 else (i, i - 1) for i in...  1.34 us
    slice x1, local copies, waits for them, and re-layouts, shards(): velocity[:, :, :EDGE]  1.07 us
  transfers between devices with their start and end apart: 7, of which 2 were waited for; matrix products, arithmetic and copies ran while one was open for 0% of the time, Pallas kernels for 37%

profile of v4, /device:TPU:8, one launch (start us, length us, event | category | flops | bytes accessed | tf_op | source)
XLA Modules:
  0.0 38.6 jit_solution(5838195678563806683)
XLA Ops:
  0.0 1.1 %fusion = (f32[2,32,8,128]{3,2,1,0:T(8,128)S(1)}, f32[2,32,8,128]{3,2,1,0:T(8,128)S(1)}) fusion(f32[2,32,128,128]{3,2,1,0:T(8,128)} %refs_0_.1), kind=kLoop, calls=%fused_computation.9 | loop fusion | bytes 1048576 | tf_op jit(solution)/shard_map/slice | solution.py:554
  1.1 0.1 collective-permute-start
  1.2 2.7 %sum_rows.1 = (f32[2,32,144,128]{3,2,1,0:T(8,128)S(1)}, f32[128,128]{1,0:T(8,128)S(1)}, f32[144,128]{1,0:T(8,128)S(1)}, f32[144,128]{1,0:T(8,128)S(1)}, f32[8,12...) custom-call(f32[2,32,128,128]{3,2,1,0:T(8,128)} %refs_0_.1, ...), custom_call_target="tpu_custom_call" | custom-call | flops 2097152 | bytes 4194304 | tf_op jit(solution)/shard_map/sum_rows/pallas_call | solution.py:523
  3.9 0.0 collective-permute-done.refs_1_.refs_0_
  3.9 0.5 %sum_slopes.1.refs_16_ = f32[136,128]{1,0:T(8,128)S(1)} custom-call(f32[2,32,16,128]{3,2,1,0:T(8,128)S(1)} %collective-permute-done.refs_1_.refs_0_, f32[128,128]{1,0:T(8,128)S(1)} %get-tuple-element.40.refs_1_, f32[144,128]{1,0:T(8,128)S(1)} %get-tuple-element.32.refs_2_.refs_5_, f32[8,128]{1,0:T(8,128)S(1)} %get-tuple-element.33.refs_3_.refs_6_.refs_7_), custom_call_target="tpu_custom_call" | custom-call | flops 131072 | bytes 262144 | tf_op jit(solution)/shard_map/sum_slopes/pallas_call | solution.py:523
  4.5 1.6 %collective-permute-start.1 = (f32[136,128]{1,0:T(8,128)S(1)}, f32[136,128]{1,0:T(8,128)S(1)}, u32[]{:S(2)}, u32[]{:S(2)}) collective-permute-start(f32[136,128]{1,0:T(8,128)S(1)} %sum_slopes.1.refs_16_), channel_id=1, source_target_pairs={{0,1},{1,0},{2,3},{3,2},{4,5},{5,4},{6,7},{7,6},{8,9},{9,8},{10,11... | collective-permute-start | bytes 208904 | tf_op jit(solution)/shard_map/ppermute | solution.py:584
  6.0 3.0 %prepare_first.1 = (f32[2,32,144,128]{3,2,1,0:T(8,128)S(1)}, f32[32,144,128]{2,1,0:T(8,128)S(1)}, f32[2,32,128,128]{3,2,1,0:T(8,128)S(1)}, f32[288,128]{1,0:T(8,...) custom-call(f32[2,32,144,128]{3,2,1,0:T(8,128)S(1)} %get-tuple-element.31.refs_0_, ...), custom_call_target="tpu_custom_call", output_to_operand_aliasing={{0}: (0, {})} | custom-call | flops 15728640 | bytes 2097152 | tf_op jit(solution)/shard_map/prepare_first/pallas_call | solution.py:523
  9.0 0.1 collective-permute-done.1.refs_8_
  9.1 1.6 %collective-permute-start.2 = (f32[136,128]{1,0:T(8,128)S(1)}, f32[136,128]{1,0:T(8,128)S(1)}, u32[]{:S(2)}, u32[]{:S(2)}) collective-permute-start(f32[136,128]{1,0:T(8,128)S(1)} %add_add_fusion.2), channel_id=1, source_target_pairs={{0,2},{1,3},{2,0},{3,1},{4,6},{5,7},{6,4},{7,5},{8,10},{9,11},{10,... | collective-permute-start | bytes 208904 | tf_op jit(solution)/shard_map/ppermute | solution.py:584
  10.7 2.9 %prepare_last.1 = (f32[32,144,128]{2,1,0:T(8,128)S(1)}, f32[2,32,128,128]{3,2,1,0:T(8,128)S(1)}, f32[288,128]{1,0:T(8,128)S(1)}, f32[288,128]{1,0:T(8,128)S(1)}, f32[136,128]{1,0:T(8,128)S(1)}) custom-call(f32[2,32,144,128]{3,2,1,0:T(8,128)S(1)} %get-tuple-element.35.refs_0_, ...), custom_call_target="tpu_custom_call", output_to_operand_aliasing={{0}: (1, {}), {1}: (2, {}), {2}: (3, {}), {3}: (4, {})} | custom-call | flops 15728640 | bytes 2097152 | tf_op jit(solution)/shard_map/prepare_last/pallas_call | solution.py:523
  13.6 0.0 collective-permute-done.2.refs_2_
  13.7 0.5 %collective-permute-start.3 = (f32[136,128]{1,0:T(8,128)S(1)}, f32[136,128]{1,0:T(8,128)S(1)}, u32[]{:S(2)}, u32[]{:S(2)}) collective-permute-start(f32[136,128]{1,0:T(8,128)S(1)} %add_add_fusion.1), channel_id=1, source_target_pairs={{0,4},{1,5},{2,6},{3,7},{4,0},{5,1},{6,2},{7,3},{8,12},{9,13},{10,... | collective-permute-start | bytes 208904 | tf_op jit(solution)/shard_map/ppermute | solution.py:584
  14.2 1.5 %collective-permute-start.4 = (f32[288,128]{1,0:T(8,128)S(1)}, f32[288,128]{1,0:T(8,128)S(1)}, u32[]{:S(2)}, u32[]{:S(2)}) collective-permute-start(f32[288,128]{1,0:T(8,128)S(1)} %get-tuple-element.48.refs_10_), channel_id=1, source_target_pairs={{0,1},{1,0},{2,3},{3,2},{4,5},{5,4},{6,7},{7,6},{8,9},{9,8},{10,11... | collective-permute-start | bytes 442376 | tf_op jit(solution)/shard_map/ppermute | solution.py:629
  15.7 2.6 %known_first.1 = (f32[2,32,128,128]{3,2,1,0:T(8,128)S(1)}, f32[3,32,144,128]{3,2,1,0:T(8,128)S(1)}, f32[3,32,128,128]{3,2,1,0:T(8,128)S(1)}, f32[136,128]{1,0:T(8,128)S(1)}) custom-call(f32[2,32,144,128]{3,2,1,0:T(8,128)S(1)} %get-tuple-element.35.refs_0_, f32[144,128]{1,0:T(8,128)S(1)} %get-tuple-element.42.refs_1_.refs_4_.refs_6_, ...), custom_call_target="tpu_custom_call" | custom-call | flops 20971520 | bytes 2097152 | tf_op jit(solution)/shard_map/known_first/pallas_call | solution.py:523
  18.3 0.0 collective-permute-done.3.refs_5_.refs_7_
  18.3 2.7 %collective-permute-start.6 = (f32[136,128]{1,0:T(8,128)S(1)}, f32[136,128]{1,0:T(8,128)S(1)}, u32[]{:S(2)}, u32[]{:S(2)}) collective-permute-start(f32[136,128]{1,0:T(8,128)S(1)} %add_add_fusion), channel_id=1, source_target_pairs={{0,8},{1,9},{2,10},{3,11},{4,12},{5,13},{6,14},{7,15},{8,0},{9,1},... | collective-permute-start | bytes 208904 | tf_op jit(solution)/shard_map/ppermute | solution.py:584
  21.0 4.2 %collective-permute-start.5 = (f32[288,128]{1,0:T(8,128)S(1)}, f32[288,128]{1,0:T(8,128)S(1)}, u32[]{:S(2)}, u32[]{:S(2)}) collective-permute-start(f32[288,128]{1,0:T(8,128)S(1)} %get-tuple-element.54.refs_11_), channel_id=1, source_target_pairs={{1,2},{2,1},{3,4},{4,3},{5,6},{6,5},{7,8},{8,7},{9,10},{10,9},{11,... | collective-permute-start | bytes 442376 | tf_op jit(solution)/shard_map/ppermute | solution.py:630
  25.2 0.0 collective-permute-done.4.refs_6_.refs_12_
  25.2 3.2 %known_last.1 = (f32[2,32,128,128]{3,2,1,0:T(8,128)S(1)}, f32[3,32,144,128]{3,2,1,0:T(8,128)S(1)}, f32[3,32,128,128]{3,2,1,0:T(8,128)S(1)}, f32[136,128]{1,0:T(8,128)}) custom-call(f32[2,32,144,128]{3,2,1,0:T(8,128)S(1)} %get-tuple-element.35.refs_0_, ...), custom_call_target="tpu_custom_call", output_to_operand_aliasing={{0}: (1, {}), {1}: (2, {}), {2}: (3, {})} | custom-call | flops 20971520 | bytes 2097152 | tf_op jit(solution)/shard_map/known_last/pallas_call | solution.py:523
  28.5 0.0 collective-permute-done.6
  28.5 1.3 %collective-permute-done.5.refs_13_ = f32[288,128]{1,0:T(8,128)S(1)} collective-permute-done((f32[288,128]{1,0:T(8,128)S(1)}, f32[288,128]{1,0:T(8,128)S(1)}, u32[]{:S(2)}, u32[]{:S(2)}) %collective-permute-start.5) | collective-permute-done | bytes 147488 | tf_op jit(solution)/shard_map/ppermute | solution.py:630
  29.8 8.8 %finish.1 = f32[3,32,128,128]{3,2,1,0:T(8,128)} custom-call(f32[2,32,144,128]{3,2,1,0:T(8,128)S(1)} %get-tuple-element.35.refs_0_, f32[32,144,128]{2,1,0:T(8,128)S(1)} %get-tuple-element.41.refs_1_, f32[2,32,128,128]{3,2,1,0:T(8,128)S(1)} %get-tuple-element.49.refs_2_, f32[2,32,128,128]{3,2,1,0:T(8,128)S(1)} %get-tuple-element.50.refs_3_, ...), custom_call_target="tpu_custom_call" | custom-call | flops 41943040 | bytes 10485760 | tf_op jit(solution)/shard_map/finish/pallas_call | solution.py:523
  (6 shorter events, 0.1 us)
Async XLA Ops:
  1.1 2.8 %collective-permute-start = (f32[2,32,16,128]{3,2,1,0:T(8,128)S(1)}, f32[2,32,16,128]{3,2,1,0:T(8,128)S(1)}, u32[]{:S(2)}, u32[]{:S(2)}) collective-permute-start(f32[2,32,16,128]{3,2,1,0:T(8,128)S(1)} %pad_maximum_fusion), channel_id=1, source_target_pairs={{0,16},{16,0},{1,17},{17,1},{2,18},{18,2},{3,19},{19,3},{4,20},{20... | collective-permute-start | bytes 1572872 | tf_op jit(solution)/shard_map/ppermute | solution.py:555
  4.5 4.6 %collective-permute-start.1 = (f32[136,128]{1,0:T(8,128)S(1)}, f32[136,128]{1,0:T(8,128)S(1)}, u32[]{:S(2)}, u32[]{:S(2)}) collective-permute-start(f32[136,128]{1,0:T(8,128)S(1)} %sum_slopes.1.refs_16_), channel_id=1, source_target_pairs={{0,1},{1,0},{2,3},{3,2},{4,5},{5,4},{6,7},{7,6},{8,9},{9,8},{10,11... | collective-permute-start | bytes 208904 | tf_op jit(solution)/shard_map/ppermute | solution.py:584
  9.1 4.5 %collective-permute-start.2 = (f32[136,128]{1,0:T(8,128)S(1)}, f32[136,128]{1,0:T(8,128)S(1)}, u32[]{:S(2)}, u32[]{:S(2)}) collective-permute-start(f32[136,128]{1,0:T(8,128)S(1)} %add_add_fusion.2), channel_id=1, source_target_pairs={{0,2},{1,3},{2,0},{3,1},{4,6},{5,7},{6,4},{7,5},{8,10},{9,11},{10,... | collective-permute-start | bytes 208904 | tf_op jit(solution)/shard_map/ppermute | solution.py:584
  13.7 4.6 %collective-permute-start.3 = (f32[136,128]{1,0:T(8,128)S(1)}, f32[136,128]{1,0:T(8,128)S(1)}, u32[]{:S(2)}, u32[]{:S(2)}) collective-permute-start(f32[136,128]{1,0:T(8,128)S(1)} %add_add_fusion.1), channel_id=1, source_target_pairs={{0,4},{1,5},{2,6},{3,7},{4,0},{5,1},{6,2},{7,3},{8,12},{9,13},{10,... | collective-permute-start | bytes 208904 | tf_op jit(solution)/shard_map/ppermute | solution.py:584
  14.2 11.0 %collective-permute-start.4 = (f32[288,128]{1,0:T(8,128)S(1)}, f32[288,128]{1,0:T(8,128)S(1)}, u32[]{:S(2)}, u32[]{:S(2)}) collective-permute-start(f32[288,128]{1,0:T(8,128)S(1)} %get-tuple-element.48.refs_10_), channel_id=1, source_target_pairs={{0,1},{1,0},{2,3},{3,2},{4,5},{5,4},{6,7},{7,6},{8,9},{9,8},{10,11... | collective-permute-start | bytes 442376 | tf_op jit(solution)/shard_map/ppermute | solution.py:629
  18.3 10.1 %collective-permute-start.6 = (f32[136,128]{1,0:T(8,128)S(1)}, f32[136,128]{1,0:T(8,128)S(1)}, u32[]{:S(2)}, u32[]{:S(2)}) collective-permute-start(f32[136,128]{1,0:T(8,128)S(1)} %add_add_fusion), channel_id=1, source_target_pairs={{0,8},{1,9},{2,10},{3,11},{4,12},{5,13},{6,14},{7,15},{8,0},{9,1},... | collective-permute-start | bytes 208904 | tf_op jit(solution)/shard_map/ppermute | solution.py:584
  21.0 8.8 %collective-permute-start.5 = (f32[288,128]{1,0:T(8,128)S(1)}, f32[288,128]{1,0:T(8,128)S(1)}, u32[]{:S(2)}, u32[]{:S(2)}) collective-permute-start(f32[288,128]{1,0:T(8,128)S(1)} %get-tuple-element.54.refs_11_), channel_id=1, source_target_pairs={{1,2},{2,1},{3,4},{4,3},{5,6},{6,5},{7,8},{8,7},{9,10},{10,9},{11,... | collective-permute-start | bytes 442376 | tf_op jit(solution)/shard_map/ppermute | solution.py:630

commit v5 on v4

--- a/solution.py
+++ b/solution.py
@@ -113,13 +113,17 @@
         bits[i : i + 1, :] = jnp.full((1, LANES), jnp.where((gy & (1 << i)) != 0, 1.0, 0.0), F32)
     lane = iota((columns, LANES), 1)
 
+    ones = jnp.ones((2 * LANES, LANES), BF16)
+
     def group(g, held):
         chunk(g).wait()
+        weighted = [pad[1, g * per + p, pl.ds(EDGE, columns), :] * rw for p in range(per)]
+        lines = jnp.dot(split(jnp.concatenate(weighted, axis=0)), ones, preferred_element_type=F32)
         for p in range(per):
             z = g * per + p
-            for c in range(2):
-                line = jnp.sum(pad[c, z, pl.ds(EDGE, columns), :] * rw, axis=1, keepdims=True)
-                held = jnp.where(lane == z + c * nz, line, held)
+            line = jnp.sum(pad[0, z, pl.ds(EDGE, columns), :] * rw, axis=1, keepdims=True)
+            held = jnp.where(lane == z, line, held)
+            held = jnp.where(lane == z + nz, lines[p * columns : (p + 1) * columns], held)
         return held
 
     uw[...] = lax.fori_loop(0, chunks, group, jnp.zeros((columns, LANES), F32))

time: 38.9 us -> 38.8 us (level)
  no operation moved by 1% of the time
where the time goes in v5:
time: 38.8 us; the launch traced here: 38.5 us
  Pallas kernels  23.6 us (61%)
  starting transfers between devices  12.1 us (31%)
  waiting for transfers between devices  1.46 us (4%)
  local copies, waits for them, and re-layouts  1.07 us (3%)
    pallas_call x7, Pallas kernels, call(): pl.pallas_call(body, name=name, in_specs=[HBM if i in far else WHOLE for...  23.6 us
    ppermute x4, starting transfers between devices, scan_step(): came = lax.ppermute(total, 'gy', [(i, i ^ 1 << level) for i in range(n_gy)])  6.32 us
    ppermute x1, starting transfers between devices, shards(): lax.ppermute(strip_b, 'gy', [(i, i + 1) if i % 2 else (i, i - 1) for i in...  4.23 us
    ppermute x1, starting transfers between devices, shards(): got_a = lax.ppermute(strip_a, 'gy', [(i, i ^ 1) for i in range(n_gy)])  1.49 us
    ppermute x1, waiting for transfers between devices, shards(): lax.ppermute(strip_b, 'gy', [(i, i + 1) if i % 2 else (i, i - 1) for i in...  1.34 us
    slice x1, local copies, waits for them, and re-layouts, shards(): velocity[:, :, :EDGE]  1.07 us
  transfers between devices with their start and end apart: 7, of which 2 were waited for; matrix products, arithmetic and copies ran while one was open for 0% of the time, Pallas kernels for 37%

profile of v5, /device:TPU:8, one launch (start us, length us, event | category | flops | bytes accessed | tf_op | source)
XLA Modules:
  0.0 38.5 jit_solution(1446976889833497133)
XLA Ops:
  0.0 1.1 %fusion = (f32[2,32,8,128]{3,2,1,0:T(8,128)S(1)}, f32[2,32,8,128]{3,2,1,0:T(8,128)S(1)}) fusion(f32[2,32,128,128]{3,2,1,0:T(8,128)} %refs_0_.1), kind=kLoop, calls=%fused_computation.9 | loop fusion | bytes 1048576 | tf_op jit(solution)/shard_map/slice | solution.py:558
  1.1 0.1 collective-permute-start
  1.2 2.6 %sum_rows.1 = (f32[2,32,144,128]{3,2,1,0:T(8,128)S(1)}, f32[128,128]{1,0:T(8,128)S(1)}, f32[144,128]{1,0:T(8,128)S(1)}, f32[144,128]{1,0:T(8,128)S(1)}, f32[8,12...) custom-call(f32[2,32,128,128]{3,2,1,0:T(8,128)} %refs_0_.1, ...), custom_call_target="tpu_custom_call" | custom-call | flops 2097152 | bytes 4194304 | tf_op jit(solution)/shard_map/sum_rows/pallas_call | solution.py:527
  3.8 0.0 collective-permute-done.refs_1_.refs_0_
  3.8 0.5 %sum_slopes.1.refs_16_ = f32[136,128]{1,0:T(8,128)S(1)} custom-call(f32[2,32,16,128]{3,2,1,0:T(8,128)S(1)} %collective-permute-done.refs_1_.refs_0_, f32[128,128]{1,0:T(8,128)S(1)} %get-tuple-element.40.refs_1_, f32[144,128]{1,0:T(8,128)S(1)} %get-tuple-element.32.refs_2_.refs_5_, f32[8,128]{1,0:T(8,128)S(1)} %get-tuple-element.33.refs_3_.refs_6_.refs_7_), custom_call_target="tpu_custom_call" | custom-call | flops 131072 | bytes 262144 | tf_op jit(solution)/shard_map/sum_slopes/pallas_call | solution.py:527
  4.4 1.6 %collective-permute-start.1 = (f32[136,128]{1,0:T(8,128)S(1)}, f32[136,128]{1,0:T(8,128)S(1)}, u32[]{:S(2)}, u32[]{:S(2)}) collective-permute-start(f32[136,128]{1,0:T(8,128)S(1)} %sum_slopes.1.refs_16_), channel_id=1, source_target_pairs={{0,1},{1,0},{2,3},{3,2},{4,5},{5,4},{6,7},{7,6},{8,9},{9,8},{10,11... | collective-permute-start | bytes 208904 | tf_op jit(solution)/shard_map/ppermute | solution.py:588
  5.9 3.0 %prepare_first.1 = (f32[2,32,144,128]{3,2,1,0:T(8,128)S(1)}, f32[32,144,128]{2,1,0:T(8,128)S(1)}, f32[2,32,128,128]{3,2,1,0:T(8,128)S(1)}, f32[288,128]{1,0:T(8,...) custom-call(f32[2,32,144,128]{3,2,1,0:T(8,128)S(1)} %get-tuple-element.31.refs_0_, ...), custom_call_target="tpu_custom_call", output_to_operand_aliasing={{0}: (0, {})} | custom-call | flops 15728640 | bytes 2097152 | tf_op jit(solution)/shard_map/prepare_first/pallas_call | solution.py:527
  8.9 0.1 collective-permute-done.1.refs_8_
  9.0 1.6 %collective-permute-start.2 = (f32[136,128]{1,0:T(8,128)S(1)}, f32[136,128]{1,0:T(8,128)S(1)}, u32[]{:S(2)}, u32[]{:S(2)}) collective-permute-start(f32[136,128]{1,0:T(8,128)S(1)} %add_add_fusion.2), channel_id=1, source_target_pairs={{0,2},{1,3},{2,0},{3,1},{4,6},{5,7},{6,4},{7,5},{8,10},{9,11},{10,... | collective-permute-start | bytes 208904 | tf_op jit(solution)/shard_map/ppermute | solution.py:588
  10.6 2.9 %prepare_last.1 = (f32[32,144,128]{2,1,0:T(8,128)S(1)}, f32[2,32,128,128]{3,2,1,0:T(8,128)S(1)}, f32[288,128]{1,0:T(8,128)S(1)}, f32[288,128]{1,0:T(8,128)S(1)}, f32[136,128]{1,0:T(8,128)S(1)}) custom-call(f32[2,32,144,128]{3,2,1,0:T(8,128)S(1)} %get-tuple-element.35.refs_0_, ...), custom_call_target="tpu_custom_call", output_to_operand_aliasing={{0}: (1, {}), {1}: (2, {}), {2}: (3, {}), {3}: (4, {})} | custom-call | flops 15728640 | bytes 2097152 | tf_op jit(solution)/shard_map/prepare_last/pallas_call | solution.py:527
  13.6 0.0 collective-permute-done.2.refs_2_
  13.6 0.5 %collective-permute-start.3 = (f32[136,128]{1,0:T(8,128)S(1)}, f32[136,128]{1,0:T(8,128)S(1)}, u32[]{:S(2)}, u32[]{:S(2)}) collective-permute-start(f32[136,128]{1,0:T(8,128)S(1)} %add_add_fusion.1), channel_id=1, source_target_pairs={{0,4},{1,5},{2,6},{3,7},{4,0},{5,1},{6,2},{7,3},{8,12},{9,13},{10,... | collective-permute-start | bytes 208904 | tf_op jit(solution)/shard_map/ppermute | solution.py:588
  14.1 1.5 %collective-permute-start.4 = (f32[288,128]{1,0:T(8,128)S(1)}, f32[288,128]{1,0:T(8,128)S(1)}, u32[]{:S(2)}, u32[]{:S(2)}) collective-permute-start(f32[288,128]{1,0:T(8,128)S(1)} %get-tuple-element.48.refs_10_), channel_id=1, source_target_pairs={{0,1},{1,0},{2,3},{3,2},{4,5},{5,4},{6,7},{7,6},{8,9},{9,8},{10,11... | collective-permute-start | bytes 442376 | tf_op jit(solution)/shard_map/ppermute | solution.py:633
  15.6 2.6 %known_first.1 = (f32[2,32,128,128]{3,2,1,0:T(8,128)S(1)}, f32[3,32,144,128]{3,2,1,0:T(8,128)S(1)}, f32[3,32,128,128]{3,2,1,0:T(8,128)S(1)}, f32[136,128]{1,0:T(8,128)S(1)}) custom-call(f32[2,32,144,128]{3,2,1,0:T(8,128)S(1)} %get-tuple-element.35.refs_0_, f32[144,128]{1,0:T(8,128)S(1)} %get-tuple-element.42.refs_1_.refs_4_.refs_6_, ...), custom_call_target="tpu_custom_call" | custom-call | flops 20971520 | bytes 2097152 | tf_op jit(solution)/shard_map/known_first/pallas_call | solution.py:527
  18.2 0.0 collective-permute-done.3.refs_5_.refs_7_
  18.3 2.7 %collective-permute-start.6 = (f32[136,128]{1,0:T(8,128)S(1)}, f32[136,128]{1,0:T(8,128)S(1)}, u32[]{:S(2)}, u32[]{:S(2)}) collective-permute-start(f32[136,128]{1,0:T(8,128)S(1)} %add_add_fusion), channel_id=1, source_target_pairs={{0,8},{1,9},{2,10},{3,11},{4,12},{5,13},{6,14},{7,15},{8,0},{9,1},... | collective-permute-start | bytes 208904 | tf_op jit(solution)/shard_map/ppermute | solution.py:588
  20.9 4.2 %collective-permute-start.5 = (f32[288,128]{1,0:T(8,128)S(1)}, f32[288,128]{1,0:T(8,128)S(1)}, u32[]{:S(2)}, u32[]{:S(2)}) collective-permute-start(f32[288,128]{1,0:T(8,128)S(1)} %get-tuple-element.54.refs_11_), channel_id=1, source_target_pairs={{1,2},{2,1},{3,4},{4,3},{5,6},{6,5},{7,8},{8,7},{9,10},{10,9},{11,... | collective-permute-start | bytes 442376 | tf_op jit(solution)/shard_map/ppermute | solution.py:634
  25.1 0.0 collective-permute-done.4.refs_6_.refs_12_
  25.2 3.2 %known_last.1 = (f32[2,32,128,128]{3,2,1,0:T(8,128)S(1)}, f32[3,32,144,128]{3,2,1,0:T(8,128)S(1)}, f32[3,32,128,128]{3,2,1,0:T(8,128)S(1)}, f32[136,128]{1,0:T(8,128)}) custom-call(f32[2,32,144,128]{3,2,1,0:T(8,128)S(1)} %get-tuple-element.35.refs_0_, ...), custom_call_target="tpu_custom_call", output_to_operand_aliasing={{0}: (1, {}), {1}: (2, {}), {2}: (3, {})} | custom-call | flops 20971520 | bytes 2097152 | tf_op jit(solution)/shard_map/known_last/pallas_call | solution.py:527
  28.4 0.0 collective-permute-done.6
  28.4 1.3 %collective-permute-done.5.refs_13_ = f32[288,128]{1,0:T(8,128)S(1)} collective-permute-done((f32[288,128]{1,0:T(8,128)S(1)}, f32[288,128]{1,0:T(8,128)S(1)}, u32[]{:S(2)}, u32[]{:S(2)}) %collective-permute-start.5) | collective-permute-done | bytes 147488 | tf_op jit(solution)/shard_map/ppermute | solution.py:634
  29.7 8.8 %finish.1 = f32[3,32,128,128]{3,2,1,0:T(8,128)} custom-call(f32[2,32,144,128]{3,2,1,0:T(8,128)S(1)} %get-tuple-element.35.refs_0_, f32[32,144,128]{2,1,0:T(8,128)S(1)} %get-tuple-element.41.refs_1_, f32[2,32,128,128]{3,2,1,0:T(8,128)S(1)} %get-tuple-element.49.refs_2_, f32[2,32,128,128]{3,2,1,0:T(8,128)S(1)} %get-tuple-element.50.refs_3_, ...), custom_call_target="tpu_custom_call" | custom-call | flops 41943040 | bytes 10485760 | tf_op jit(solution)/shard_map/finish/pallas_call | solution.py:527
  (6 shorter events, 0.1 us)
Async XLA Ops:
  1.1 2.7 %collective-permute-start = (f32[2,32,16,128]{3,2,1,0:T(8,128)S(1)}, f32[2,32,16,128]{3,2,1,0:T(8,128)S(1)}, u32[]{:S(2)}, u32[]{:S(2)}) collective-permute-start(f32[2,32,16,128]{3,2,1,0:T(8,128)S(1)} %pad_maximum_fusion), channel_id=1, source_target_pairs={{0,16},{16,0},{1,17},{17,1},{2,18},{18,2},{3,19},{19,3},{4,20},{20... | collective-permute-start | bytes 1572872 | tf_op jit(solution)/shard_map/ppermute | solution.py:559
  4.4 4.6 %collective-permute-start.1 = (f32[136,128]{1,0:T(8,128)S(1)}, f32[136,128]{1,0:T(8,128)S(1)}, u32[]{:S(2)}, u32[]{:S(2)}) collective-permute-start(f32[136,128]{1,0:T(8,128)S(1)} %sum_slopes.1.refs_16_), channel_id=1, source_target_pairs={{0,1},{1,0},{2,3},{3,2},{4,5},{5,4},{6,7},{7,6},{8,9},{9,8},{10,11... | collective-permute-start | bytes 208904 | tf_op jit(solution)/shard_map/ppermute | solution.py:588
  9.0 4.5 %collective-permute-start.2 = (f32[136,128]{1,0:T(8,128)S(1)}, f32[136,128]{1,0:T(8,128)S(1)}, u32[]{:S(2)}, u32[]{:S(2)}) collective-permute-start(f32[136,128]{1,0:T(8,128)S(1)} %add_add_fusion.2), channel_id=1, source_target_pairs={{0,2},{1,3},{2,0},{3,1},{4,6},{5,7},{6,4},{7,5},{8,10},{9,11},{10,... | collective-permute-start | bytes 208904 | tf_op jit(solution)/shard_map/ppermute | solution.py:588
  13.6 4.6 %collective-permute-start.3 = (f32[136,128]{1,0:T(8,128)S(1)}, f32[136,128]{1,0:T(8,128)S(1)}, u32[]{:S(2)}, u32[]{:S(2)}) collective-permute-start(f32[136,128]{1,0:T(8,128)S(1)} %add_add_fusion.1), channel_id=1, source_target_pairs={{0,4},{1,5},{2,6},{3,7},{4,0},{5,1},{6,2},{7,3},{8,12},{9,13},{10,... | collective-permute-start | bytes 208904 | tf_op jit(solution)/shard_map/ppermute | solution.py:588
  14.1 11.1 %collective-permute-start.4 = (f32[288,128]{1,0:T(8,128)S(1)}, f32[288,128]{1,0:T(8,128)S(1)}, u32[]{:S(2)}, u32[]{:S(2)}) collective-permute-start(f32[288,128]{1,0:T(8,128)S(1)} %get-tuple-element.48.refs_10_), channel_id=1, source_target_pairs={{0,1},{1,0},{2,3},{3,2},{4,5},{5,4},{6,7},{7,6},{8,9},{9,8},{10,11... | collective-permute-start | bytes 442376 | tf_op jit(solution)/shard_map/ppermute | solution.py:633
  18.3 10.1 %collective-permute-start.6 = (f32[136,128]{1,0:T(8,128)S(1)}, f32[136,128]{1,0:T(8,128)S(1)}, u32[]{:S(2)}, u32[]{:S(2)}) collective-permute-start(f32[136,128]{1,0:T(8,128)S(1)} %add_add_fusion), channel_id=1, source_target_pairs={{0,8},{1,9},{2,10},{3,11},{4,12},{5,13},{6,14},{7,15},{8,0},{9,1},... | collective-permute-start | bytes 208904 | tf_op jit(solution)/shard_map/ppermute | solution.py:588
  20.9 8.8 %collective-permute-start.5 = (f32[288,128]{1,0:T(8,128)S(1)}, f32[288,128]{1,0:T(8,128)S(1)}, u32[]{:S(2)}, u32[]{:S(2)}) collective-permute-start(f32[288,128]{1,0:T(8,128)S(1)} %get-tuple-element.54.refs_11_), channel_id=1, source_target_pairs={{1,2},{2,1},{3,4},{4,3},{5,6},{6,5},{7,8},{8,7},{9,10},{10,9},{11,... | collective-permute-start | bytes 442376 | tf_op jit(solution)/shard_map/ppermute | solution.py:634
